TPU v7x, 128 devices: a whole 4x4x4 slice. The times are simulated.
128 devices in a mesh: wide: 16 (over x, y_lo, core), narrow: 8 (over z, y_hi).
Axes of the slice: x: 4, y: 4 (y_hi: 2, y_lo: 2; y = y_hi * 2 + y_lo), z: 4, core: 2. Of those that a mesh axis runs over, the one named last changes fastest.
Arguments:
- tokens: bfloat16 [16384, 2048], P(('wide', 'narrow')), may hold values from -6 to 6
- cotangent: bfloat16 [16384, 2048], P(('wide', 'narrow')), may hold values from -6 to 6
- doc_lengths: int32 [16, 3], P('wide'), may hold values from 1 to 1022, as said below
- pre_gain: float32 [2048], replicated, may hold values from 0.1 to 1.9
- mid_gain: float32 [2048], replicated, may hold values from 0.1 to 1.9
- query_gain: float32 [128], replicated, may hold values from 0.1 to 1.9
- key_gain: float32 [128], replicated, may hold values from 0.1 to 1.9
- query_weight: bfloat16 [2048, 2048], P(None, 'narrow'), may hold values from -0.125 to 0.125
- key_matrix: bfloat16 [2048, 1024], P(None, 'narrow'), may hold values from -0.125 to 0.125
- value_matrix: bfloat16 [2048, 1024], P(None, 'narrow'), may hold values from -0.125 to 0.125
- output_weight: bfloat16 [2048, 2048], P('narrow'), may hold values from -1 to 1
- gate_weight: bfloat16 [2048, 6144], P(None, 'narrow'), may hold values from -0.125 to 0.125
- up_weight: bfloat16 [2048, 6144], P(None, 'narrow'), may hold values from -0.125 to 0.125
- down_weight: bfloat16 [6144, 2048], P('narrow'), may hold values from -0.078125 to 0.078125
Outputs:
- block_output: bfloat16 [16384, 2048], P(('wide', 'narrow'))
- tokens_grad: bfloat16 [16384, 2048], P(('wide', 'narrow'))
- pregain_grad: float32 [2048], P('wide')
- midgain_grad: float32 [2048], P('wide')
- querygain_grad: float32 [128], P('wide')
- keygain_grad: float32 [128], P('wide')
- query_grad: float32 [2048, 2048], P('wide', 'narrow')
- key_grad: float32 [2048, 1024], P('wide', 'narrow')
- value_grad: float32 [2048, 1024], P('wide', 'narrow')
- output_grad: float32 [2048, 2048], P('narrow', 'wide')
- gate_grad: float32 [2048, 6144], P('wide', 'narrow')
- up_grad: float32 [2048, 6144], P('wide', 'narrow')
- down_grad: float32 [6144, 2048], P('narrow', 'wide')
Inputs may be any that keep to these rules, and one draw needn't show every extreme that they name: `doc_lengths`: each row's 3 lengths sum to 1024; in every row one document starts among its first 128 places and ends among its last 128.
All inputs are finite; a program needn't handle non-finite values.
Results may differ from a plain program's by a relative error of at most 0.04.
Values may be sent and summed in bfloat16 or wider, within the bound.
No kernel may reach another device: no remote copies, remote signals or barrier semaphores. Data moves between devices by JAX's collectives and lax.ppermute only.
A program may use at most 192 MiB of HBM per device.

v0:
```python
import math

import jax
import jax.numpy as jnp
from jax import lax
from jax.sharding import Mesh
from jax.sharding import PartitionSpec as P

NARROW = ("narrow_0", "narrow_1")
WIDE_NARROW = ("wide", "narrow_0", "narrow_1")


norm_eps = 1e-06
rope_base = 1000000.0


def summed_rows(terms, axes):
    so_far = terms.astype(jnp.bfloat16)
    for axis in axes:
        so_far = lax.psum_scatter(so_far, axis, scatter_dimension=0, tiled=True)
    return so_far.astype(jnp.float32)


def side_by_side(arrays, axis, dim, along):
    both = jnp.concatenate(arrays, axis=along)
    out, at, finished = (lax.psum_scatter(both, axis, scatter_dimension=dim, tiled=True), 0, [])
    for a in arrays:
        finished.append(lax.slice_in_dim(out, at, at + a.shape[along], axis=along))
        at += a.shape[along]
    return tuple(finished)


def from_everyone(shard, axis):
    copies = jnp.broadcast_to(shard, (lax.axis_size(axis), *shard.shape))
    return lax.all_to_all(copies, axis, split_axis=0, concat_axis=0, tiled=True)


def of_everyone(shard, axis):
    return from_everyone(shard, axis).sum(axis=0)


def in_one(arrays, axis):
    line, at, finished = (jnp.concatenate([a.reshape(-1) for a in arrays]), 0, [])
    so_far = of_everyone(line, axis)
    for a in arrays:
        finished.append(so_far[at : at + a.size].reshape(a.shape))
        at += a.size
    return tuple(finished)


def rms_apply(values, gain):
    inverse = lax.rsqrt(jnp.mean(values * values, axis=-1, keepdims=True) + norm_eps)
    return values * inverse * gain


def rotary(values, cosine, sine):
    half = values.shape[-1] // 2
    first = values[..., :half]
    second = values[..., half:]
    cos_part = cosine[..., None, :]
    sin_part = sine[..., None, :]
    return jnp.concatenate(
        [first * cos_part - second * sin_part, second * cos_part + first * sin_part], axis=-1
    )


def row_tables(lengths, row_len, head_dim):
    ends = jnp.cumsum(lengths)
    starts = ends - lengths
    places = jnp.arange(row_len, dtype=jnp.int32)
    begin = jnp.max(jnp.where(starts[None, :] <= places[:, None], starts[None, :], 0), axis=1)
    offset = (places - begin).astype(jnp.float32)
    half = head_dim // 2
    freq = jnp.exp(jnp.arange(half, dtype=jnp.float32) * (-2.0 * math.log(rope_base) / head_dim))
    angle = offset[:, None] * freq[None, :]
    return (begin, jnp.cos(angle), jnp.sin(angle))


def head_prep(raw, gain, cosine, sine, heads):
    shaped = raw.reshape(raw.shape[0], heads, -1)
    return rotary(rms_apply(shaped, gain), cosine, sine)


def span_mask(places, begin, first, span):
    rows_at = first + jnp.arange(span, dtype=jnp.int32)
    begin_part = lax.dynamic_slice_in_dim(begin, first, span, 0)
    return (places[None, :] <= rows_at[:, None]) & (places[None, :] >= begin_part[:, None])


def span_scores(query_part, key_low, visible, scale):
    scores = (
        jnp.einsum("sagd,tad->agst", query_part, key_low, preferred_element_type=jnp.float32)
        * scale
    )
    return jnp.where(visible, scores, -1e30)


def attention_forward(query_low, key_low, value_reduced, begin, scale):
    total = key_low.shape[0]
    span = min(512, total)
    places = jnp.arange(total, dtype=jnp.int32)

    def one_span(index):
        first = index * span
        query_part = lax.dynamic_slice_in_dim(query_low, first, span, 0)
        scores = span_scores(query_part, key_low, span_mask(places, begin, first, span), scale)
        peak = jnp.max(scores, axis=-1, keepdims=True)
        expo = jnp.exp(scores - peak)
        summed = jnp.sum(expo, axis=-1, keepdims=True)
        weights = (expo / summed).astype(jnp.bfloat16)
        context = jnp.einsum(
            "agst,tad->sagd", weights, value_reduced, preferred_element_type=jnp.float32
        )
        return (context.astype(jnp.bfloat16), (peak + jnp.log(summed))[..., 0])

    context, logsum = lax.map(one_span, jnp.arange(total // span, dtype=jnp.int32))
    return (context.reshape(total, -1), logsum)


def attention_backward(query_low, key_low, value_reduced, begin, logsum, dcontext, scale):
    total = key_low.shape[0]
    span = min(512, total)
    places = jnp.arange(total, dtype=jnp.int32)

    def one_span(carry, inputs):
        dkey_sum, dvalue_sum = carry
        index, logsum_part = inputs
        first = index * span
        query_part = lax.dynamic_slice_in_dim(query_low, first, span, 0)
        dcontext_part = lax.dynamic_slice_in_dim(dcontext, first, span, 0)
        scores = span_scores(query_part, key_low, span_mask(places, begin, first, span), scale)
        weights = jnp.exp(scores - logsum_part[..., None])
        dweights = jnp.einsum(
            "sagd,tad->agst", dcontext_part, value_reduced, preferred_element_type=jnp.float32
        )
        inner = jnp.sum(weights * dweights, axis=-1, keepdims=True)
        dscores = (scale * weights * (dweights - inner)).astype(jnp.bfloat16)
        dquery_part = jnp.einsum(
            "agst,tad->sagd", dscores, key_low, preferred_element_type=jnp.float32
        )
        dkey_sum = dkey_sum + jnp.einsum(
            "agst,sagd->tad", dscores, query_part, preferred_element_type=jnp.float32
        )
        dvalue_sum = dvalue_sum + jnp.einsum(
            "agst,sagd->tad",
            weights.astype(jnp.bfloat16),
            dcontext_part,
            preferred_element_type=jnp.float32,
        )
        return ((dkey_sum, dvalue_sum), dquery_part)

    zeros = jnp.zeros(key_low.shape, jnp.float32)
    (dkey_sum, dvalue_sum), dquery = lax.scan(
        one_span, (zeros, zeros), (jnp.arange(total // span, dtype=jnp.int32), logsum)
    )
    return (dquery.reshape(total, -1, key_low.shape[-1]), dkey_sum, dvalue_sum)


def body(
    tokens,
    cotangent,
    doc_lengths,
    pre_gain,
    mid_gain,
    query_gain,
    key_gain,
    query_weight,
    key_matrix,
    value_matrix,
    output_weight,
    gate_weight,
    up_weight,
    down_weight,
):
    seg_rows = tokens.shape[0]
    head_dim = query_gain.shape[0]
    query_heads = query_weight.shape[1] // head_dim
    kv_heads = key_matrix.shape[1] // head_dim
    group_size = query_heads // kv_heads
    row_len = seg_rows * lax.axis_size(NARROW)
    scale = head_dim ** (-0.5)
    begin, cosine, sine = row_tables(doc_lengths[0], row_len, head_dim)
    resid_in = tokens.astype(jnp.float32)
    normed_before = rms_apply(resid_in, pre_gain).astype(jnp.bfloat16)
    normed_full = lax.all_gather(normed_before, NARROW, axis=0, tiled=True)
    query_raw = jnp.dot(normed_full, query_weight, preferred_element_type=jnp.float32)
    unrotated_key = jnp.dot(normed_full, key_matrix, preferred_element_type=jnp.float32)
    value_reduced = (
        jnp.dot(normed_full, value_matrix, preferred_element_type=jnp.float32)
        .astype(jnp.bfloat16)
        .reshape(row_len, kv_heads, head_dim)
    )
    query_low = (
        head_prep(query_raw, query_gain, cosine, sine, query_heads)
        .astype(jnp.bfloat16)
        .reshape(row_len, kv_heads, group_size, head_dim)
    )
    key_low = head_prep(unrotated_key, key_gain, cosine, sine, kv_heads).astype(jnp.bfloat16)
    context_low, logsum = attention_forward(query_low, key_low, value_reduced, begin, scale)
    first_state = (query_raw, unrotated_key, query_low, key_low, value_reduced, context_low, logsum)
    context_first = first_state[5]
    attended = lax.psum_scatter(
        jnp.dot(context_first, output_weight, preferred_element_type=jnp.float32).astype(
            jnp.bfloat16
        ),
        NARROW,
        scatter_dimension=0,
        tiled=True,
    ).astype(jnp.float32)
    hidden = resid_in + attended
    mid_normed = rms_apply(hidden, mid_gain).astype(jnp.bfloat16)
    mid_full = lax.all_gather(mid_normed, NARROW, axis=0, tiled=True)
    gate_value = jnp.dot(mid_full, gate_weight, preferred_element_type=jnp.float32)
    upper_value = jnp.dot(mid_full, up_weight, preferred_element_type=jnp.float32)
    product_low = (jax.nn.silu(gate_value) * upper_value).astype(jnp.bfloat16)
    mixed = lax.psum_scatter(
        jnp.dot(product_low, down_weight, preferred_element_type=jnp.float32).astype(jnp.bfloat16),
        NARROW,
        scatter_dimension=0,
        tiled=True,
    ).astype(jnp.float32)
    block_output = (hidden + mixed).astype(jnp.bfloat16)
    upstream = cotangent.astype(jnp.float32)
    upstream_full = lax.all_gather(cotangent, NARROW, axis=0, tiled=True)
    down_grad = jnp.einsum(
        "tf,td->fd", product_low, upstream_full, preferred_element_type=jnp.float32
    )
    dproduct = jnp.einsum(
        "td,fd->tf", upstream_full, down_weight, preferred_element_type=jnp.float32
    )
    unused_act, pull_act = jax.vjp(
        lambda gate_in, upper_in: jax.nn.silu(gate_in) * upper_in, gate_value, upper_value
    )
    dgate, dupper = pull_act(dproduct)
    dgate_low = dgate.astype(jnp.bfloat16)
    dupper_low = dupper.astype(jnp.bfloat16)
    gate_grad = jnp.einsum("td,tf->df", mid_full, dgate_low, preferred_element_type=jnp.float32)
    up_grad = jnp.einsum("td,tf->df", mid_full, dupper_low, preferred_element_type=jnp.float32)
    dmid = summed_rows(
        jnp.einsum("tf,df->td", dgate_low, gate_weight, preferred_element_type=jnp.float32)
        + jnp.einsum("tf,df->td", dupper_low, up_weight, preferred_element_type=jnp.float32),
        NARROW,
    )
    unused_mid, pull_mid = jax.vjp(rms_apply, hidden, mid_gain)
    dhidden_norm, mid_part = pull_mid(dmid)
    dhidden = upstream + dhidden_norm
    dattended_full = lax.all_gather(dhidden.astype(jnp.bfloat16), NARROW, axis=0, tiled=True)
    query_raw, unrotated_key, query_low, key_low, value_reduced, context_low, logsum = first_state
    output_grad = jnp.einsum(
        "tc,td->cd", context_low, dattended_full, preferred_element_type=jnp.float32
    )
    dcontext = (
        jnp.einsum("td,cd->tc", dattended_full, output_weight, preferred_element_type=jnp.float32)
        .astype(jnp.bfloat16)
        .reshape(row_len, kv_heads, group_size, head_dim)
    )
    dquery_rot, dkey_rot, dvalue = attention_backward(
        query_low, key_low, value_reduced, begin, logsum, dcontext, scale
    )
    dvalue_low = dvalue.reshape(row_len, -1).astype(jnp.bfloat16)
    unused_query, pull_query = jax.vjp(
        lambda raw, gain: head_prep(raw, gain, cosine, sine, query_heads), query_raw, query_gain
    )
    dquery_raw, querygain_part = pull_query(dquery_rot)
    unused_key, pull_key = jax.vjp(
        lambda raw, gain: head_prep(raw, gain, cosine, sine, kv_heads), unrotated_key, key_gain
    )
    dkey_raw, keygain_part = pull_key(dkey_rot)
    dquery_low = dquery_raw.astype(jnp.bfloat16)
    dkey_low = dkey_raw.astype(jnp.bfloat16)
    query_grad = jnp.einsum(
        "td,tc->dc", normed_full, dquery_low, preferred_element_type=jnp.float32
    )
    key_grad = jnp.einsum("td,tc->dc", normed_full, dkey_low, preferred_element_type=jnp.float32)
    value_grad = jnp.einsum(
        "td,tc->dc", normed_full, dvalue_low, preferred_element_type=jnp.float32
    )
    dpre = lax.psum_scatter(
        (
            jnp.einsum("tc,dc->td", dquery_low, query_weight, preferred_element_type=jnp.float32)
            + jnp.einsum("tc,dc->td", dkey_low, key_matrix, preferred_element_type=jnp.float32)
            + jnp.einsum("tc,dc->td", dvalue_low, value_matrix, preferred_element_type=jnp.float32)
        ).astype(jnp.bfloat16),
        NARROW,
        scatter_dimension=0,
        tiled=True,
    ).astype(jnp.float32)
    unused_pre, pull_pre = jax.vjp(rms_apply, resid_in, pre_gain)
    dtokens_norm, pre_part = pull_pre(dpre)
    tokens_grad = (dhidden + dtokens_norm).astype(jnp.bfloat16)
    everything = (
        *tuple(
            (
                part.astype(jnp.float32)
                for part in side_by_side(
                    (
                        query_grad.astype(jnp.bfloat16),
                        key_grad.astype(jnp.bfloat16),
                        value_grad.astype(jnp.bfloat16),
                    ),
                    "wide",
                    0,
                    1,
                )
            )
        ),
        lax.psum_scatter(
            output_grad.astype(jnp.bfloat16), "wide", scatter_dimension=1, tiled=True
        ).astype(jnp.float32),
        *tuple(
            (
                part.astype(jnp.float32)
                for part in side_by_side(
                    (gate_grad.astype(jnp.bfloat16), up_grad.astype(jnp.bfloat16)), "wide", 0, 1
                )
            )
        ),
        lax.psum_scatter(
            down_grad.astype(jnp.bfloat16), "wide", scatter_dimension=1, tiled=True
        ).astype(jnp.float32),
        lax.psum_scatter(
            pre_part.astype(jnp.bfloat16), "wide", scatter_dimension=0, tiled=True
        ).astype(jnp.float32),
        lax.psum_scatter(
            mid_part.astype(jnp.bfloat16), "wide", scatter_dimension=0, tiled=True
        ).astype(jnp.float32),
        lax.psum_scatter(
            querygain_part.astype(jnp.bfloat16), "wide", scatter_dimension=0, tiled=True
        ).astype(jnp.float32),
        lax.psum_scatter(
            keygain_part.astype(jnp.bfloat16), "wide", scatter_dimension=0, tiled=True
        ).astype(jnp.float32),
    )
    (
        query_sum,
        key_sum,
        value_sum,
        output_sum,
        gate_sum,
        upper_sum,
        down_sum,
        pre_sum,
        mid_sum,
        querygain_sum,
        keygain_sum,
    ) = everything
    pregain_grad, midgain_grad, querygain_grad, keygain_grad = in_one(
        (pre_sum, mid_sum, querygain_sum, keygain_sum), NARROW
    )
    return (
        block_output,
        tokens_grad,
        pregain_grad,
        midgain_grad,
        querygain_grad,
        keygain_grad,
        query_sum,
        key_sum,
        value_sum,
        output_sum,
        gate_sum,
        upper_sum,
        down_sum,
    )


def solution(mesh):
    torus = Mesh(mesh.devices.reshape(mesh.shape["wide"], 4, 2), ("wide", "narrow_0", "narrow_1"))
    return jax.shard_map(
        body,
        mesh=torus,
        in_specs=(
            P(WIDE_NARROW, None),
            P(WIDE_NARROW, None),
            P("wide", None),
            P(),
            P(),
            P(),
            P(),
            P(None, NARROW),
            P(None, NARROW),
            P(None, NARROW),
            P(NARROW, None),
            P(None, NARROW),
            P(None, NARROW),
            P(NARROW, None),
        ),
        out_specs=(
            P(WIDE_NARROW, None),
            P(WIDE_NARROW, None),
            P("wide"),
            P("wide"),
            P("wide"),
            P("wide"),
            P("wide", NARROW),
            P("wide", NARROW),
            P("wide", NARROW),
            P(NARROW, "wide"),
            P("wide", NARROW),
            P("wide", NARROW),
            P(NARROW, "wide"),
        ),
        check_vma=False,
    )
```

profile of v0, /device:TPU:0, one launch (start us, length us, event | category | flops | bytes accessed | tf_op | source)
XLA Modules:
  0.0 981.1 jit_solution(7114064729420286636)
XLA Ops:
  8.7 2.0 fusion.71
  12.4 3.1 multiply_cosine_fusion
  15.5 69.6 %all-gather.5.cloned.1.call-done = bf16[1024,2048]{1,0:T(8,128)(2,1)} async-done(((bf16[128,2048]{1,0:T(8,128)(2,1)}), bf16[1024,2048]{1,0:T(8,128)(2,1)}) %all-gather.5.cloned.1.call-update) | async-done | bytes 4194320 | tf_op jit(solution)/shard_map/all_gather | solution.py:185
  85.0 3.8 multiply_reduce_fusion.4
  92.7 4.8 multiply_reduce_fusion.3
  97.5 2.6 copy.90
  100.1 1.7 multiply_multiply_fusion
  101.9 1.7 fusion.82
  104.6 2.0 fusion.70
  106.6 15.9 %while.30 = (s32[]{:T(128)}, bf16[2,512,1,2,128]{4,3,1,0,2:T(2,128)(2,1)}, f32[2,1,2,512]{3,2,1,0:T(2,128)S(1)}, s32[2]{0:T(128)S(1)}, s32[1024]{0:T(1024)S(1)},...) while((s32[]{:T(128)}, ...), condition=%wide.region_8.9_spmd.clone.clone, body=%wide.region_5.8_spmd.clone.clone.sunk | while | flops 551157248 | bytes 21539104 | solution.py:116
  108.5 2.1 fusion.187
  116.5 2.1 fusion.187
  122.5 4.6 convolution_convert_fusion
  127.2 82.5 %reduce-scatter.18.cloned.1.call-done = bf16[128,2048]{1,0:T(8,128)(2,1)} async-done(((bf16[1024,2048]{1,0:T(8,128)(2,1)}), bf16[128,2048]{1,0:T(8,128)(2,1)}) %reduce-scatter.18.cloned.1.call-update) | async-done | bytes 524304 | tf_op jit(solution)/shard_map/reduce_scatter | solution.py:202
  211.2 2.2 multiply_convert_fusion.2
  214.5 69.4 %all-gather.7.cloned.1.call-done = bf16[1024,2048]{1,0:T(8,128)(2,1)} async-done(((bf16[128,2048]{1,0:T(8,128)(2,1)}), bf16[1024,2048]{1,0:T(8,128)(2,1)}) %all-gather.7.cloned.1.call-update) | async-done | bytes 4194320 | tf_op jit(solution)/shard_map/all_gather | solution.py:212
  283.9 8.3 fusion.120
  292.3 5.1 fusion.119
  297.3 58.4 %all-gather.9.cloned.1.call-done = bf16[1024,2048]{1,0:T(8,128)(2,1)} async-done(((bf16[128,2048]{1,0:T(8,128)(2,1)}), bf16[1024,2048]{1,0:T(8,128)(2,1)}) %all-gather.9.cloned.1.call-update) | async-done | bytes 4194320 | tf_op jit(solution)/shard_map/all_gather | solution.py:224
  355.7 9.8 %multiply_convert_fusion = (bf16[1024,768]{1,0:T(8,128)(2,1)S(1)}, bf16[1024,768]{1,0:T(8,128)(2,1)S(1)}, bf16[1024,768]{1,0:T(8,128)(2,1)}) fusion(f32[1024,768]{1,0:T(8,128)} %fusion.119, f32[1024,768]{1,0:T(8,128)} %fusion.120, bf16[1024,2048]{1,0:T(8,128)(2,1)} %all-gather.9.cloned.1.call-done, bf16[768,2048]{1,0:T(8,128)(2,1)S(1)} %copy-done), kind=kOutput, calls=%fused_computation.80 | convolution fusion | flops 3233808384 | bytes 18350080 | tf_op jit(solution)/shard_map/td,fd->tf/dot_general | solution.py:228
  365.6 3.5 fusion.121
  369.1 5.2 add_convert_fusion.1
  374.4 44.9 %reduce-scatter.22.cloned.1.call-done = bf16[256,2048]{1,0:T(8,128)(2,1)} async-done(((bf16[1024,2048]{1,0:T(8,128)(2,1)}), bf16[256,2048]{1,0:T(8,128)(2,1)}) %reduce-scatter.22.cloned.1.call-update) | async-done | bytes 1048592 | tf_op jit(solution)/shard_map/reduce_scatter | solution.py:20
  419.3 26.1 %reduce-scatter.24.cloned.1.call-done = bf16[128,2048]{1,0:T(8,128)(2,1)} async-done(((bf16[256,2048]{1,0:T(8,128)(2,1)}), bf16[128,2048]{1,0:T(8,128)(2,1)}) %reduce-scatter.24.cloned.1.call-update) | async-done | bytes 524304 | tf_op jit(solution)/shard_map/reduce_scatter | solution.py:20
  445.4 1.8 fusion.73
  447.3 2.8 fusion.114
  450.1 7.8 convolution_convert_fusion.2
  457.9 4.8 copy.113
  462.8 6.3 convolution_convert_fusion.3
  469.1 3.9 convolution_convert_fusion.4
  473.0 3.8 pad_maximum_fusion
  476.7 8.6 copy.111
  485.7 35.6 %all-gather.11.cloned.1.call-done = bf16[1024,2048]{1,0:T(8,128)(2,1)} async-done(((bf16[128,2048]{1,0:T(8,128)(2,1)}), bf16[1024,2048]{1,0:T(8,128)(2,1)}) %all-gather.11.cloned.1.call-update) | async-done | bytes 4194320 | tf_op jit(solution)/shard_map/all_gather | solution.py:247
  521.2 4.6 convolution_convert_fusion.6
  525.8 2.2 copy.109
  528.1 4.7 convolution_convert_fusion.9
  532.8 22.0 %while.31 = (s32[]{:T(128)}, f32[1024,1,128]{0,2,1:T(8,128)}, f32[1024,1,128]{0,2,1:T(8,128)}, f32[2,512,1,2,128]{4,1,0,3,2:T(8,128)}, s32[2]{0:T(128)S(1)}, /*i...) while((s32[]{:T(128)}, f32[1024,1,128]{0,2,1:T(8,128)}, ...), condition=%wide.region_17.18_spmd.clone.clone, body=%wide.region_15.17_spmd.clone.clone.sunk | while | flops 1361051136 | bytes 60070388 | solution.py:153
  534.7 1.7 fusion.198
  537.9 2.0 fusion.200
  545.7 1.7 fusion.198
  548.9 2.0 fusion.200
  554.7 2.3 multiply_add_fusion.1
  558.0 1.7 fusion.76
  560.1 2.8 fusion.102
  562.9 2.1 copy.98
  566.5 1.6 fusion.104
  568.1 3.0 convolution_convert_fusion.8
  574.7 3.9 copy.107
  578.7 2.4 fusion.122
  582.6 3.4 add_convert_fusion
  586.1 6.4 convolution_convert_fusion.1
  596.9 67.0 %reduce-scatter.32.cloned.1.call-done = bf16[128,1536]{1,0:T(8,128)(2,1)} async-done(((bf16[2048,1536]{1,0:T(8,128)(2,1)}), bf16[128,1536]{1,0:T(8,128)(2,1)}) %reduce-scatter.32.cloned.1.call-update) | async-done | bytes 393232
  663.9 1.7 fusion.115
  665.6 1.7 copy.129
  667.4 1.8 copy.104
  670.0 1.8 copy.103
  671.8 57.3 %reduce-scatter.30.cloned.1.call-done = bf16[128,256]{1,0:T(8,128)(2,1)} async-done(((bf16[2048,256]{1,0:T(8,128)(2,1)}), bf16[128,256]{1,0:T(8,128)(2,1)}) %reduce-scatter.30.cloned.1.call-update) | async-done | bytes 65552
  730.8 63.4 %reduce-scatter.28.cloned.1.call-done = bf16[128,512]{1,0:T(8,128)(2,1)} async-done(((bf16[2048,512]{1,0:T(8,128)(2,1)}), bf16[128,512]{1,0:T(8,128)(2,1)}) %reduce-scatter.28.cloned.1.call-update) | async-done | bytes 131088
  798.4 82.7 %reduce-scatter.26.cloned.1.call-done = bf16[128,2048]{1,0:T(8,128)(2,1)} async-done(((bf16[1024,2048]{1,0:T(8,128)(2,1)}), bf16[128,2048]{1,0:T(8,128)(2,1)}) %reduce-scatter.26.cloned.1.call-update) | async-done | bytes 524304 | tf_op jit(solution)/shard_map/reduce_scatter | solution.py:278
  881.1 1.8 fusion.74
  882.9 29.6 %all-reduce.8 = (bf16[128]{0:T(256)(128)(2,1)S(1)}, bf16[128]{0:T(256)(128)(2,1)S(1)}, bf16[2048]{0:T(1024)(128)(2,1)S(1)}, bf16[2048]{0:T(1024)(128)(2,1)S(1)}) all-reduce(bf16[128]{0:T(256)(128)(2,1)S(1)} %get-tuple-element.408, ...), channel_id=10, replica_groups=mesh['wide'=16,'narrow_0'=4,'narrow_1'=2] {'wide'}, use_global_device_ids=true, to_apply=%region_29.30.clone | all-reduce | flops 4352 | bytes 17408
  913.5 4.5 all-to-all-start
  918.0 51.3 %reduce-scatter.20.cloned.1.call-done = bf16[128,2048]{1,0:T(8,128)(2,1)} async-done(((bf16[1024,2048]{1,0:T(8,128)(2,1)}), bf16[128,2048]{1,0:T(8,128)(2,1)}) %reduce-scatter.20.cloned.1.call-update) | async-done | bytes 524304 | tf_op jit(solution)/shard_map/reduce_scatter | solution.py:216
  969.4 3.7 fusion.78
  (254 shorter events, 54.2 us)
Async XLA Ops:
  7.2 348.6 %copy-start = (bf16[768,2048]{1,0:T(8,128)(2,1)S(1)}, bf16[768,2048]{1,0:T(8,128)(2,1)}, u32[]{:S(2)}) copy-start(bf16[768,2048]{1,0:T(8,128)(2,1)} %param.31) | copy-start | bytes 9437188
  7.2 82.4 %copy-start.37 = (f32[128]{0:T(128)S(1)}, f32[128]{0:T(128)}, u32[]{:S(2)}) copy-start(f32[128]{0:T(128)} %param.24) | copy-start | bytes 1540
  7.2 77.8 %all-gather.5.cloned.1.call-start = ((), (), s32[]{:S(2)}) async-start(), calls=%async_computation.10 | async-start | bytes 4718592 | tf_op jit(solution)/shard_map/all_gather | solution.py:185
  8.6 80.3 %copy-start.45 = (f32[128]{0:T(128)}, f32[128]{0:T(128)S(1)}, u32[]{:S(2)}) copy-start(f32[128]{0:T(128)S(1)} %fusion.79) | copy-start | bytes 1540
  8.6 80.2 %copy-start.41 = (f32[128]{0:T(128)}, f32[128]{0:T(128)S(1)}, u32[]{:S(2)}) copy-start(f32[128]{0:T(128)S(1)} %fusion.112) | copy-start | bytes 1540
  10.7 199.0 %reduce-scatter.18.cloned.1.call-start = ((), (), s32[]{:S(2)}) async-start(), calls=%async_computation.11 | async-start | bytes 4718592 | tf_op jit(solution)/shard_map/reduce_scatter | solution.py:202
  11.6 80.0 %copy-start.39 = (f32[64]{0:T(128)}, f32[64]{0:T(128)S(1)}, u32[]{:S(2)}) copy-start(f32[64]{0:T(128)S(1)} %multiply_exponential_fusion) | copy-start | bytes 772
  12.4 79.2 %copy-start.31 = (f32[1024]{0:T(1024)}, f32[1024]{0:T(1024)S(1)}, u32[]{:S(2)}) copy-start(f32[1024]{0:T(1024)S(1)} %subtract_convert_fusion.1) | copy-start | bytes 12292
  88.9 2.0 copy-start.7
  88.9 15.7 %copy-start.33 = (f32[1024]{0:T(1024)}, f32[1024]{0:T(1024)S(1)}, u32[]{:S(2)}) copy-start(f32[1024]{0:T(1024)S(1)} %get-tuple-element.481) | copy-start | bytes 12292
  92.7 7.4 copy-start.43
  97.5 6.0 copy-start.35
  100.1 4.5 copy-start.1
  100.1 4.5 copy-start.23
  100.1 1.7 copy-start.26
  108.5 3.3 copy-start.8
  116.5 3.3 copy-start.8
  127.1 84.1 %copy-start.25 = (f32[2048]{0:T(1024)S(1)}, f32[2048]{0:T(1024)}, u32[]{:S(2)}) copy-start(f32[2048]{0:T(1024)} %param.22) | copy-start | bytes 24580
  127.1 156.8 %all-gather.7.cloned.1.call-start = ((), (), s32[]{:S(2)}) async-start(), calls=%async_computation.12 | async-start | bytes 4718592 | tf_op jit(solution)/shard_map/all_gather | solution.py:212
  213.4 142.3 %all-gather.9.cloned.1.call-start = ((), (), s32[]{:S(2)}) async-start(), calls=%async_computation.14 | async-start | bytes 4718592 | tf_op jit(solution)/shard_map/all_gather | solution.py:224
  214.0 205.2 %reduce-scatter.22.cloned.1.call-start = ((), (), s32[]{:S(2)}) async-start(), calls=%async_computation.15 | async-start | bytes 5242880 | tf_op jit(solution)/shard_map/reduce_scatter | solution.py:20
  283.9 8.3 copy-start.47
  283.9 8.3 copy-start.49
  355.7 9.9 %copy-start.50 = (bf16[2048,768]{1,0:T(8,128)(2,1)S(1)}, bf16[2048,768]{1,0:T(8,128)(2,1)}, u32[]{:S(2)}) copy-start(bf16[2048,768]{1,0:T(8,128)(2,1)} %param.29) | copy-start | bytes 9437188
  365.6 3.5 copy-start.53
  365.6 3.5 copy-start.55
  365.6 3.5 copy-start.51
  374.3 71.1 %reduce-scatter.24.cloned.1.call-start = ((), (), s32[]{:S(2)}) async-start(), calls=%async_computation.16 | async-start | bytes 1572864 | tf_op jit(solution)/shard_map/reduce_scatter | solution.py:20
  419.3 102.0 %all-gather.11.cloned.1.call-start = ((), (), s32[]{:S(2)}) async-start(), calls=%async_computation.17 | async-start | bytes 4718592 | tf_op jit(solution)/shard_map/all_gather | solution.py:247
  450.1 145.0 %reduce-scatter.34.cloned.1.call-start = ((), (), s32[]{:S(2)}) async-start(), calls=%async_computation.22 | async-start | bytes 3342336
  462.7 201.2 %reduce-scatter.32.cloned.1.call-start = ((), (), s32[]{:S(2)}) async-start(), calls=%async_computation.21 | async-start | bytes 6684672
  462.8 6.3 copy-start.48
  462.8 6.3 copy-start.54
  485.4 243.8 %reduce-scatter.30.cloned.1.call-start = ((), (), s32[]{:S(2)}) async-start(), calls=%async_computation.20 | async-start | bytes 1114112
  534.0 2.4 copy-start.12
  534.0 2.4 copy-start.13
  537.9 2.0 copy-start.14
  539.9 2.0 copy-start.10
  545.0 2.4 copy-start.12
  545.0 2.4 copy-start.13
  548.9 2.0 copy-start.14
  550.9 2.0 copy-start.10
  554.7 2.3 copy-start.6
  554.7 2.3 copy-start.27
  554.7 2.3 copy-start.44
  554.7 3.3 copy-start.36
  557.0 3.1 copy-start.32
  557.0 3.1 copy-start.40
  558.0 7.0 copy-start.30
  558.0 7.0 copy-start.38
  558.0 8.4 copy-start.34
  559.8 234.4 %reduce-scatter.28.cloned.1.call-start = ((), (), s32[]{:S(2)}) async-start(), calls=%async_computation.19 | async-start | bytes 2228224
  562.9 3.6 copy-start.17
  565.0 6.1 copy-start.2
  565.0 6.1 copy-start.15
  568.1 3.7 copy-start.18
  578.6 302.5 %reduce-scatter.26.cloned.1.call-start = ((), (), s32[]{:S(2)}) async-start(), calls=%async_computation.18 | async-start | bytes 4718592 | tf_op jit(solution)/shard_map/reduce_scatter | solution.py:278
  578.7 2.4 copy-start.16
  578.7 2.4 copy-start.24
  586.0 383.3 %reduce-scatter.20.cloned.1.call-start = ((), (), s32[]{:S(2)}) async-start(), calls=%async_computation.13 | async-start | bytes 4718592 | tf_op jit(solution)/shard_map/reduce_scatter | solution.py:216
  592.5 288.6 %copy-start.28 = (f32[2048]{0:T(1024)S(1)}, f32[2048]{0:T(1024)}, u32[]{:S(2)}) copy-start(f32[2048]{0:T(1024)} %param.21) | copy-start | bytes 24580
  592.5 288.6 %copy-start.42 = (f32[128]{0:T(128)S(1)}, f32[128]{0:T(128)}, u32[]{:S(2)}) copy-start(f32[128]{0:T(128)} %copy-done.41) | copy-start | bytes 1540
  592.5 325.5 %copy-start.46 = (f32[128]{0:T(128)S(1)}, f32[128]{0:T(128)}, u32[]{:S(2)}) copy-start(f32[128]{0:T(128)} %copy-done.45) | copy-start | bytes 1540
  913.5 59.5 %all-to-all-start = ((f32[8,1,272]{2,1,0:T(1,128)}), f32[8,1,272]{2,1,0:T(1,128)S(1)}, u32[]{:S(2)}, u32[]{:S(2)}) async-start(f32[8,1,272]{2,1,0:T(1,128)} %broadcast_in_dim.73), calls=%async_computation.5 | async-start | bytes 24576 | tf_op jit(solution)/shard_map/all_to_all | solution.py:35
  (18 other events, 21.5 us)
Sparse Core Ops, SparseCore 0:
  11.0 74.0 all-gather.4
  127.3 82.4 reduce-scatter.17
  213.5 70.3 all-gather.6
  286.4 69.2 all-gather.8
  374.5 44.7 reduce-scatter.21
  421.5 23.9 reduce-scatter.23
  450.2 70.9 all-gather.10
  523.8 63.2 reduce-scatter.33
  589.6 74.2 reduce-scatter.31
  666.3 62.8 reduce-scatter.29
  731.6 62.5 reduce-scatter.27
  797.8 83.2 reduce-scatter.25
  885.4 83.8 reduce-scatter.19
where the time goes:
time: 991 us; the launch traced here: 981 us
  waiting for transfers between devices  709 us (72%)
  matrix products  113 us (11%)
  other arithmetic  53.6 us (5%)
  local copies, waits for them, and re-layouts  50.8 us (5%)
  blocking collectives  29.6 us (3%)
  between operations  16.3 us (2%)
    unnamed x17, waiting for transfers between devices  188 us
    reduce_scatter x1, waiting for transfers between devices, body(): lax.psum_scatter((jnp.einsum('tc,dc->td', dquery_low, query_weight, prefe...  82.7 us
    reduce_scatter x1, waiting for transfers between devices, body(): lax.psum_scatter(jnp.dot(context_first, output_weight, preferred_element_...  82.5 us
    reduce_scatter x2, waiting for transfers between devices, summed_rows(): so_far = lax.psum_scatter(so_far, axis, scatter_dimension=0, tiled=True)  71 us
    all_gather x1, waiting for transfers between devices, body(): normed_full = lax.all_gather(normed_before, NARROW, axis=0, tiled=True)  69.6 us
    all_gather x1, waiting for transfers between devices, body(): mid_full = lax.all_gather(mid_normed, NARROW, axis=0, tiled=True)  69.4 us
    all_gather x1, waiting for transfers between devices, body(): upstream_full = lax.all_gather(cotangent, NARROW, axis=0, tiled=True)  58.4 us
    reduce_scatter x1, waiting for transfers between devices, body(): lax.psum_scatter(jnp.dot(product_low, down_weight, preferred_element_type...  51.3 us
  transfers between devices with their start and end apart: 14, of which 12 were waited for; matrix products, arithmetic and copies ran while one was open for 15% of the time, Pallas kernels for 0%

commit v1 on v0

v1 whole, which is shorter than its diff:
```python
import math

import jax
import jax.numpy as jnp
from jax import lax
from jax.experimental import pallas as pl
from jax.experimental.pallas import tpu as pltpu
from jax.sharding import Mesh
from jax.sharding import PartitionSpec as P

NARROW = ("z", "yhi")
WIDE = ("x", "ylo", "core")
ALL = WIDE + NARROW

EPS = 1e-06
ROPE_BASE = 1000000.0
LOG2E = math.log2(math.e)
F32 = jnp.float32
BF16 = jnp.bfloat16


def dot(a, b, ca, cb):
    return lax.dot_general(a, b, (((ca,), (cb,)), ((), ())), preferred_element_type=F32)


def gather_z(piece):
    copies = jnp.broadcast_to(piece, (4, *piece.shape))
    out = lax.all_to_all(copies, "z", split_axis=0, concat_axis=0, tiled=True)
    return out.reshape(-1, piece.shape[-1])


def scatter_z(partial):
    pieces = partial.reshape(4, -1, partial.shape[-1])
    out = lax.all_to_all(pieces, "z", split_axis=0, concat_axis=0, tiled=True)
    return out.astype(F32).sum(axis=0)


def swap(v, axis):
    return lax.ppermute(v, axis, [(0, 1), (1, 0)])


def cross(v):
    return lax.ppermute(v, ("ylo", "yhi"), [(0, 3), (3, 0), (1, 2), (2, 1)])


def partner_weights(ordered):
    x = lax.axis_index("x")
    piece = lax.dynamic_slice_in_dim(ordered[:1024], x * 256, 256, 0)
    first = lax.all_gather(cross(piece), "x", axis=0, tiled=True)
    second = swap(first, "core")
    return jnp.concatenate([first, second], axis=0)


def wide_sum(keep, send):
    c = keep.shape[1] // 2
    got = swap(send, "core")
    half = (keep.astype(F32) + got.astype(F32)).astype(BF16)
    quarter = lax.psum_scatter(half, "x", scatter_dimension=0, tiled=True).reshape(2, 128, 2 * c)
    ylo = lax.axis_index("ylo")
    mine = lax.dynamic_index_in_dim(quarter, ylo, 0, keepdims=False)
    other = lax.dynamic_index_in_dim(quarter, 1 - ylo, 0, keepdims=False)
    total = mine[:, :c].astype(F32) + swap(other[:, :c], "ylo").astype(F32)
    total = total + swap(mine[:, c:], "yhi").astype(F32)
    return total + cross(other[:, c:]).astype(F32)


def rope(v, cosine, sine):
    return v * cosine + pltpu.roll(v, 64, 1) * sine


def rope_back(v, cosine, sine):
    return v * cosine - pltpu.roll(v, 64, 1) * sine


def vmem_spec():
    return pl.BlockSpec(memory_space=pltpu.VMEM)


def smem_spec():
    return pl.BlockSpec(memory_space=pltpu.SMEM)


def prep_kernel(raw_ref, cos_ref, sin_ref, qgain_ref, kgain_ref, q_ref, kv_ref):
    cosine, sine = cos_ref[...], sin_ref[...]

    def prep(raw, gain):
        inverse = lax.rsqrt(jnp.mean(raw * raw, axis=1, keepdims=True) + EPS)
        return rope(raw * inverse * gain, cosine, sine).astype(BF16)

    for g in range(2):
        at = 512 * g
        for h in range(2):
            q_ref[:, 256 * g + 128 * h : 256 * g + 128 * (h + 1)] = prep(
                raw_ref[:, at + 128 * h : at + 128 * (h + 1)], qgain_ref[...]
            )
        kv_ref[:, 256 * g : 256 * g + 128] = prep(raw_ref[:, at + 256 : at + 384], kgain_ref[...])
        kv_ref[:, 256 * g + 128 : 256 * g + 256] = raw_ref[:, at + 384 : at + 512].astype(BF16)


def prepare(raw, cosine, sine, qgain, kgain):
    return pl.pallas_call(
        prep_kernel,
        out_shape=(
            jax.ShapeDtypeStruct((512, 512), BF16),
            jax.ShapeDtypeStruct((512, 512), BF16),
        ),
        in_specs=[vmem_spec()] * 5,
        out_specs=[vmem_spec()] * 2,
        compiler_params=pltpu.CompilerParams(vmem_limit_bytes=40 * 2**20),
        cost_estimate=pl.CostEstimate(
            flops=10_000_000, bytes_accessed=4_000_000, transcendentals=10_000
        ),
        name="prepare",
    )(raw, cosine, sine, qgain, kgain)


def place_keys(y, kv_ref, other_ref, k_all, v_all):
    for g in range(2):
        for z in range(4):
            rows = slice(128 * z, 128 * (z + 1))
            at = pl.ds(pl.multiple_of(256 * z + 128 * y, 128), 128)
            bt = pl.ds(pl.multiple_of(256 * z + 128 * (1 - y), 128), 128)
            k_all[g, at, :] = kv_ref[rows, 256 * g : 256 * g + 128]
            v_all[g, at, :] = kv_ref[rows, 256 * g + 128 : 256 * g + 256]
            og = 256 * (1 - g)
            k_all[g, bt, :] = other_ref[rows, og : og + 128]
            v_all[g, bt, :] = other_ref[rows, og + 128 : og + 256]


def seen_by(y, z, begin):
    rows = 256 * (z + 1)
    key = lax.broadcasted_iota(jnp.int32, (rows, 256), 0)
    query = (lax.broadcasted_iota(jnp.int32, (rows, 256), 1) & 127) + (256 * z + 128 * y)
    return (key <= query) & (key >= begin)


def stacked(ref, z, g):
    rows = slice(128 * z, 128 * (z + 1))
    return jnp.concatenate(
        [ref[rows, 256 * g : 256 * g + 128], ref[rows, 256 * g + 128 : 256 * g + 256]], axis=0
    )


def attention_kernel(y_ref, q_ref, kv_ref, other_ref, begin_ref, ctx_ref, lse_ref, k_all, v_all):
    scale2 = 128**-0.5 * LOG2E
    y = y_ref[0]
    place_keys(y, kv_ref, other_ref, k_all, v_all)
    for g in range(2):
        v_t = v_all[g].T
        for z in range(4):
            rows = 256 * (z + 1)
            begin = begin_ref[:, 128 * z : 128 * (z + 1)]
            begin = jnp.concatenate([begin, begin], axis=1)
            s = dot(k_all[g, :rows, :], stacked(q_ref, z, g), 1, 1) * scale2
            s = jnp.where(seen_by(y, z, begin), s, -1e30)
            peak = jnp.max(s, axis=0, keepdims=True)
            expo = jnp.exp2(s - peak)
            total = jnp.sum(expo, axis=0, keepdims=True)
            weights = (expo * (1.0 / total)).astype(BF16)
            ctx = dot(v_t[:, :rows], weights, 1, 0).T.astype(BF16)
            for h in range(2):
                ctx_ref[
                    128 * z : 128 * (z + 1), 256 * g + 128 * h : 256 * g + 128 * (h + 1)
                ] = ctx[128 * h : 128 * (h + 1), :]
            lse_ref[4 * g + z : 4 * g + z + 1, :] = peak + jnp.log2(total)


def attention(y, q, kv, other, begin_row):
    return pl.pallas_call(
        attention_kernel,
        out_shape=(
            jax.ShapeDtypeStruct((512, 512), BF16),
            jax.ShapeDtypeStruct((8, 256), F32),
        ),
        in_specs=[smem_spec()] + [vmem_spec()] * 4,
        out_specs=[vmem_spec()] * 2,
        scratch_shapes=[pltpu.VMEM((2, 1024, 128), BF16), pltpu.VMEM((2, 1024, 128), BF16)],
        compiler_params=pltpu.CompilerParams(vmem_limit_bytes=40 * 2**20),
        cost_estimate=pl.CostEstimate(
            flops=900_000_000, bytes_accessed=3_000_000, transcendentals=1_400_000
        ),
        name="attention",
    )(y, q, kv, other, begin_row)


def head_back(d, raw, gain, cosine, sine):
    dn = rope_back(d, cosine, sine)
    inverse = lax.rsqrt(jnp.mean(raw * raw, axis=1, keepdims=True) + EPS)
    n = raw * inverse
    dgain = jnp.sum(dn * n, axis=0, keepdims=True)
    dn = dn * gain
    draw = inverse * (dn - n * jnp.mean(dn * n, axis=1, keepdims=True))
    return draw.astype(BF16), dgain


def attention_back_kernel(
    y_ref, q_ref, kv_ref, other_ref, begin_ref, lse_ref, dctx_ref, raw_ref, cos_ref, sin_ref,
    qgain_ref, dq_ref, mine_ref, send_ref, dqgain_ref, k_all, v_all, dk_acc, dv_acc, dq_acc,
):
    scale = 128**-0.5
    scale2 = scale * LOG2E
    y = y_ref[0]
    place_keys(y, kv_ref, other_ref, k_all, v_all)
    dk_acc[...] = jnp.zeros_like(dk_acc)
    dv_acc[...] = jnp.zeros_like(dv_acc)
    for g in range(2):
        k_t = k_all[g].T
        for z in range(4):
            rows = 256 * (z + 1)
            begin = begin_ref[:, 128 * z : 128 * (z + 1)]
            begin = jnp.concatenate([begin, begin], axis=1)
            q = stacked(q_ref, z, g)
            dctx = stacked(dctx_ref, z, g)
            s = dot(k_all[g, :rows, :], q, 1, 1) * scale2
            s = s - lse_ref[4 * g + z : 4 * g + z + 1, :]
            probs = jnp.where(seen_by(y, z, begin), jnp.exp2(s), 0.0)
            dprobs = dot(v_all[g, :rows, :], dctx, 1, 1)
            inner = jnp.sum(probs * dprobs, axis=0, keepdims=True)
            dscores = (probs * (dprobs - inner) * scale).astype(BF16)
            dv_acc[g, :rows, :] += dot(probs.astype(BF16), dctx, 1, 0)
            dk_acc[g, :rows, :] += dot(dscores, q, 1, 0)
            dq = dot(k_t[:, :rows], dscores, 1, 0).T
            for h in range(2):
                dq_acc[
                    128 * z : 128 * (z + 1), 256 * g + 128 * h : 256 * g + 128 * (h + 1)
                ] = dq[128 * h : 128 * (h + 1), :]
    dgain = jnp.zeros((1, 128), F32)
    for g in range(2):
        for h in range(2):
            lanes = slice(256 * g + 128 * h, 256 * g + 128 * (h + 1))
            raws = slice(512 * g + 128 * h, 512 * g + 128 * (h + 1))
            d, part = head_back(
                dq_acc[:, lanes], raw_ref[:, raws], qgain_ref[...], cos_ref[...], sin_ref[...]
            )
            dq_ref[:, lanes] = d
            dgain = dgain + part
        for z in range(4):
            rows = slice(128 * z, 128 * (z + 1))
            at = pl.ds(pl.multiple_of(256 * z + 128 * y, 128), 128)
            bt = pl.ds(pl.multiple_of(256 * z + 128 * (1 - y), 128), 128)
            mine_ref[rows, 256 * g : 256 * g + 128] = dk_acc[g, at, :]
            mine_ref[rows, 256 * g + 128 : 256 * g + 256] = dv_acc[g, at, :]
            send_ref[rows, 256 * g : 256 * g + 128] = dk_acc[g, bt, :].astype(BF16)
            send_ref[rows, 256 * g + 128 : 256 * g + 256] = dv_acc[g, bt, :].astype(BF16)
    dqgain_ref[...] = dgain


def attention_back(y, q, kv, other, begin_row, lse, dctx, raw, cosine, sine, qgain):
    return pl.pallas_call(
        attention_back_kernel,
        out_shape=(
            jax.ShapeDtypeStruct((512, 512), BF16),
            jax.ShapeDtypeStruct((512, 512), F32),
            jax.ShapeDtypeStruct((512, 512), BF16),
            jax.ShapeDtypeStruct((1, 128), F32),
        ),
        in_specs=[smem_spec()] + [vmem_spec()] * 10,
        out_specs=[vmem_spec()] * 4,
        scratch_shapes=[
            pltpu.VMEM((2, 1024, 128), BF16),
            pltpu.VMEM((2, 1024, 128), BF16),
            pltpu.VMEM((2, 1024, 128), F32),
            pltpu.VMEM((2, 1024, 128), F32),
            pltpu.VMEM((512, 512), F32),
        ],
        compiler_params=pltpu.CompilerParams(vmem_limit_bytes=40 * 2**20),
        cost_estimate=pl.CostEstimate(
            flops=2_200_000_000, bytes_accessed=7_000_000, transcendentals=1_400_000
        ),
        name="attention_back",
    )(y, q, kv, other, begin_row, lse, dctx, raw, cosine, sine, qgain)


def key_back_kernel(
    mine_ref, got_ref, dq_ref, raw_ref, cos_ref, sin_ref, kgain_ref, draw_ref, dkgain_ref
):
    dgain = jnp.zeros((1, 128), F32)
    for g in range(2):
        at, og = 512 * g, 256 * (1 - g)
        draw_ref[:, at : at + 256] = dq_ref[:, 256 * g : 256 * g + 256]
        dk = mine_ref[:, 256 * g : 256 * g + 128] + got_ref[:, og : og + 128].astype(F32)
        d, part = head_back(
            dk, raw_ref[:, at + 256 : at + 384], kgain_ref[...], cos_ref[...], sin_ref[...]
        )
        draw_ref[:, at + 256 : at + 384] = d
        dgain = dgain + part
        dv = mine_ref[:, 256 * g + 128 : 256 * g + 256] + got_ref[:, og + 128 : og + 256].astype(
            F32
        )
        draw_ref[:, at + 384 : at + 512] = dv.astype(BF16)
    dkgain_ref[...] = dgain


def key_back(mine, got, dq, raw, cosine, sine, kgain):
    return pl.pallas_call(
        key_back_kernel,
        out_shape=(
            jax.ShapeDtypeStruct((512, 1024), BF16),
            jax.ShapeDtypeStruct((1, 128), F32),
        ),
        in_specs=[vmem_spec()] * 7,
        out_specs=[vmem_spec()] * 2,
        compiler_params=pltpu.CompilerParams(vmem_limit_bytes=40 * 2**20),
        cost_estimate=pl.CostEstimate(
            flops=10_000_000, bytes_accessed=6_000_000, transcendentals=10_000
        ),
        name="key_back",
    )(mine, got, dq, raw, cosine, sine, kgain)


def row_tables(lengths):
    ends = jnp.cumsum(lengths)
    starts = ends - lengths
    at = jnp.arange(512, dtype=jnp.int32)
    places = (at // 128) * 256 + at % 128 + lax.axis_index("yhi") * 128
    begin = jnp.max(jnp.where(starts[None, :] <= places[:, None], starts[None, :], 0), axis=1)
    offset = (places - begin).astype(F32)
    freq = jnp.exp(jnp.arange(64, dtype=F32) * (-2.0 * math.log(ROPE_BASE) / 128))
    angle = offset[:, None] * freq[None, :]
    cosine, sine = jnp.cos(angle), jnp.sin(angle)
    return (
        begin,
        jnp.concatenate([cosine, cosine], axis=1),
        jnp.concatenate([-sine, sine], axis=1),
    )


def inverse_rms(v):
    return lax.rsqrt(jnp.mean(v * v, axis=-1, keepdims=True) + EPS)


def norm_back(d, v, inverse, gain):
    n = v * inverse
    dn = d * gain
    return inverse * (dn - n * jnp.mean(dn * n, axis=-1, keepdims=True))


def body(
    tokens, cotangent, doc_lengths, pre_gain, mid_gain, query_gain, key_gain,
    query_weight, key_matrix, value_matrix, output_weight, gate_weight, up_weight, down_weight,
):
    core = lax.axis_index("core")

    def order(v, axis):
        shape = v.shape
        parts = v.reshape(*shape[:axis], 8, 2, 128, *shape[axis + 1 :])
        even = lax.index_in_dim(parts, 0, axis + 1, keepdims=False)
        odd = lax.index_in_dim(parts, 1, axis + 1, keepdims=False)
        first = jnp.where(core == 0, even, odd)
        second = jnp.where(core == 0, odd, even)
        return jnp.concatenate([first, second], axis=axis).reshape(shape)

    def unorder(v):
        parts = v.reshape(v.shape[0], 2, 8, 128)
        first, second = parts[:, 0], parts[:, 1]
        even = jnp.where(core == 0, first, second)
        odd = jnp.where(core == 0, second, first)
        return jnp.stack([even, odd], axis=2).reshape(v.shape)

    x = order(tokens, 1).astype(F32)
    cot_low = order(cotangent, 1)
    cot = cot_low.astype(F32)
    pre_gain_o = order(pre_gain, 0)
    mid_gain_o = order(mid_gain, 0)

    r1 = inverse_rms(x)
    normed = (x * r1 * pre_gain_o).astype(BF16)
    normed_half = gather_z(normed)

    def both(own):
        ordered = order(own, 0)
        return jnp.concatenate([ordered, partner_weights(ordered)], axis=1)

    qkv_weight = both(jnp.concatenate([query_weight, key_matrix, value_matrix], axis=1))
    out = both(output_weight.T)
    gu_weight = both(jnp.concatenate([gate_weight, up_weight], axis=1))
    down = both(down_weight.T)
    begin, cosine, sine = row_tables(doc_lengths[0])
    begin_row = begin[None, :]
    qg, kg = query_gain[None, :], key_gain[None, :]
    y = lax.axis_index("yhi").reshape(1).astype(jnp.int32)

    raw = jnp.dot(normed_half, qkv_weight, preferred_element_type=F32)
    q, kv = prepare(raw, cosine, sine, qg, kg)
    kv_other = swap(kv, "yhi")
    ctx, lse = attention(y, q, kv, kv_other, begin_row)
    cot_half = gather_z(cot_low)
    attended = scatter_z(dot(ctx, out, 1, 1).astype(BF16))
    hidden = x + attended
    r2 = inverse_rms(hidden)
    mid = (hidden * r2 * mid_gain_o).astype(BF16)
    mid_half = gather_z(mid)

    gu = jnp.dot(mid_half, gu_weight, preferred_element_type=F32)
    gate = jnp.concatenate([gu[:, :768], gu[:, 1536:2304]], axis=1)
    up = jnp.concatenate([gu[:, 768:1536], gu[:, 2304:]], axis=1)
    sig = jax.nn.sigmoid(gate)
    silu = gate * sig
    product = (silu * up).astype(BF16)
    dproduct = dot(cot_half, down, 1, 0)
    dgate = (dproduct * up * sig * (1.0 + gate * (1.0 - sig))).astype(BF16)
    dup = (dproduct * silu).astype(BF16)
    dgu = jnp.concatenate([dgate[:, :768], dup[:, :768], dgate[:, 768:], dup[:, 768:]], axis=1)
    dmid = scatter_z(dot(dgu, gu_weight, 1, 1).astype(BF16))
    mixed = scatter_z(dot(product, down, 1, 1).astype(BF16))
    block_output = unorder((hidden + mixed).astype(BF16))

    def weight_grad(a, b):
        send = dot(a[:, 1024:], b, 0, 0).astype(BF16)
        keep = dot(a[:, :1024], b, 0, 0).astype(BF16)
        return wide_sum(keep, send)

    down_grad = weight_grad(cot_half, product).T
    gu_grad = weight_grad(mid_half, dgu)

    dhidden = cot + norm_back(dmid, hidden, r2, mid_gain_o)
    datt_half = gather_z(dhidden.astype(BF16))
    dctx = dot(datt_half, out, 1, 0).astype(BF16)
    dq, dkv_mine, dkv_send, dqgain = attention_back(
        y, q, kv, kv_other, begin_row, lse, dctx, raw, cosine, sine, qg
    )
    draw, dkgain = key_back(dkv_mine, swap(dkv_send, "yhi"), dq, raw, cosine, sine, kg)
    dpre = scatter_z(dot(draw, qkv_weight, 1, 1).astype(BF16))
    out_grad = weight_grad(datt_half, ctx).T
    qkv_grad = weight_grad(normed_half, draw)
    tokens_grad = unorder((dhidden + norm_back(dpre, x, r1, pre_gain_o)).astype(BF16))

    w = (lax.axis_index("x") * 2 + lax.axis_index("ylo")) * 2 + core

    def gain_part(grad, weights, gain):
        total = 0.0
        at = 0
        for weight in weights:
            c = weight.shape[1]
            block = lax.dynamic_slice_in_dim(weight, w * 128, 128, 0).astype(F32)
            total = total + jnp.sum(block * grad[:, at : at + c], axis=1)
            at += c
        return total / lax.dynamic_slice_in_dim(gain, w * 128, 128, 0)

    pre_part = gain_part(qkv_grad, (query_weight, key_matrix, value_matrix), pre_gain)
    mid_part = gain_part(gu_grad, (gate_weight, up_weight), mid_gain)
    heads = jnp.concatenate([dqgain.reshape(16, 8), dkgain.reshape(16, 8)], axis=1)
    heads = lax.all_to_all(heads, WIDE, split_axis=0, concat_axis=0, tiled=True).sum(axis=0)
    line = jnp.concatenate([pre_part, mid_part, heads])
    lines = jnp.broadcast_to(line, (8, line.shape[0]))
    line = lax.all_to_all(lines, NARROW, split_axis=0, concat_axis=0, tiled=True).sum(axis=0)

    return (
        block_output,
        tokens_grad,
        line[:128],
        line[128:256],
        line[256:264],
        line[264:272],
        qkv_grad[:, :256],
        qkv_grad[:, 256:384],
        qkv_grad[:, 384:],
        out_grad,
        gu_grad[:, :768],
        gu_grad[:, 768:],
        down_grad,
    )


def solution(mesh):
    torus = Mesh(mesh.devices.reshape(4, 2, 2, 4, 2), ("x", "ylo", "core", "z", "yhi"))
    return jax.shard_map(
        body,
        mesh=torus,
        in_specs=(
            P(ALL, None),
            P(ALL, None),
            P(WIDE, None),
            P(),
            P(),
            P(),
            P(),
            P(None, NARROW),
            P(None, NARROW),
            P(None, NARROW),
            P(NARROW, None),
            P(None, NARROW),
            P(None, NARROW),
            P(NARROW, None),
        ),
        out_specs=(
            P(ALL, None),
            P(ALL, None),
            P(WIDE),
            P(WIDE),
            P(WIDE),
            P(WIDE),
            P(WIDE, NARROW),
            P(WIDE, NARROW),
            P(WIDE, NARROW),
            P(NARROW, WIDE),
            P(WIDE, NARROW),
            P(WIDE, NARROW),
            P(NARROW, WIDE),
        ),
        check_vma=False,
    )
```

time: 991 us -> 512 us (0.52)
  waiting for transfers between devices: 709 us -> 141 us
  starting transfers between devices: 6 us -> 70.5 us
  blocking collectives: 29.6 us -> 44.7 us
  matrix products: 113 us -> 100 us
  Pallas kernels: 0 us -> 12.7 us
    reduce_scatter x5 -> x4, waiting for transfers between devices: 288 us -> 0.04 us  [wide_sum(): lax.psum_scatter(half, 'x', scatter_dimension=0, tiled=True)]
    all_gather x4 -> x3, waiting for transfers between devices: 233 us -> 10 us  [partner_weights(): first = lax.all_gather(cross(piece), 'x', axis=0, tiled=True)]
    unnamed x17 -> x7, waiting for transfers between devices: 188 us -> 0.12 us
    all_to_all x1 -> x9, waiting for transfers between devices: 0.01 us -> 97.4 us  [the longest x4 49.9 us: gather_z(): out = lax.all_to_all(copies, 'z', split_axis=0, concat_axis=0, tiled=True)]
    all_to_all x1 -> x9, starting transfers between devices: 4.53 us -> 41.1 us  [the longest x4 18.9 us: gather_z(): out = lax.all_to_all(copies, 'z', split_axis=0, concat_axis=0, tiled=True)]
    ppermute x0 -> x26, waiting for transfers between devices: none -> 33.3 us  [the longest x18 18 us: swap(): return lax.ppermute(v, axis, [(0, 1), (1, 0)])]
    unnamed x1 -> x0, blocking collectives: 29.6 us -> none
    ppermute x0 -> x26, starting transfers between devices: none -> 29 us  [the longest x18 16 us: swap(): return lax.ppermute(v, axis, [(0, 1), (1, 0)])]
  transfers between devices with their start and end apart: 14 -> 42, of which waited for: 12 -> 21; matrix products, arithmetic and copies ran while one was open for 15% -> 35% of each run, Pallas kernels for 0% -> 3%
where the time goes in v1:
time: 512 us; the launch traced here: 503 us
  waiting for transfers between devices  141 us (28%)
  matrix products  100 us (20%)
  starting transfers between devices  70.5 us (14%)
  other arithmetic  60.5 us (12%)
  local copies, waits for them, and re-layouts  57.7 us (11%)
  blocking collectives  44.7 us (9%)
  between operations  15.6 us (3%)
  Pallas kernels  12.7 us (2%)
    dot_general x14, matrix products, dot(): lax.dot_general(a, b, (((ca,), (cb,)), ((), ())), preferred_element_type=...  82.6 us
    all_to_all x4, waiting for transfers between devices, gather_z(): out = lax.all_to_all(copies, 'z', split_axis=0, concat_axis=0, tiled=True)  49.9 us
    all_to_all x3, waiting for transfers between devices, scatter_z(): out = lax.all_to_all(pieces, 'z', split_axis=0, concat_axis=0, tiled=True)  40.5 us
    all_to_all x1, blocking collectives, scatter_z(): out = lax.all_to_all(pieces, 'z', split_axis=0, concat_axis=0, tiled=True)  28.8 us
    unnamed x100, local copies, waits for them, and re-layouts  18.9 us
    all_to_all x4, starting transfers between devices, gather_z(): out = lax.all_to_all(copies, 'z', split_axis=0, concat_axis=0, tiled=True)  18.9 us
    ppermute x18, waiting for transfers between devices, swap(): return lax.ppermute(v, axis, [(0, 1), (1, 0)])  18 us
    all_gather x1, blocking collectives, partner_weights(): first = lax.all_gather(cross(piece), 'x', axis=0, tiled=True)  16 us
  transfers between devices with their start and end apart: 42, of which 21 were waited for; matrix products, arithmetic and copies ran while one was open for 35% of the time, Pallas kernels for 3%

profile of v1, /device:TPU:0, one launch (start us, length us, event | category | flops | bytes accessed | tf_op | source)
XLA Modules:
  0.0 502.9 jit_solution(9558620583750685558)
XLA Ops:
  10.0 3.1 collective-permute-start
  13.1 2.4 pad_maximum_fusion
  15.8 2.3 copy-done.10
  24.5 2.6 copy.300
  31.0 5.4 %all-to-all-start = ((bf16[4,128,2048]{2,1,0:T(8,128)(2,1)}), bf16[4,128,2048]{2,1,0:T(8,128)(2,1)}, u32[]{:S(2)}, u32[]{:S(2)}) async-start(bf16[4,128,2048]{2,1,0:T(8,128)(2,1)} %broadcast_in_dim.43), calls=%async_computation | async-start | bytes 4194304 | tf_op jit(solution)/shard_map/all_to_all | solution.py:28
  36.4 2.3 copy.260
  38.7 2.1 select_bitcast_fusion.1
  42.3 3.0 collective-permute-start.3
  45.6 8.1 %all-gather.4.cloned.1.call-done = bf16[1024,512]{1,0:T(8,128)(2,1)} async-done(((bf16[256,512]{1,0:T(8,128)(2,1)}), bf16[1024,512]{1,0:T(8,128)(2,1)}) %all-gather.4.cloned.1.call-update) | async-done | bytes 1048592 | tf_op jit(solution)/shard_map/all_gather | solution.py:49
  56.8 5.8 %all-to-all-done = bf16[4,128,2048]{2,1,0:T(8,128)(2,1)} async-done(((bf16[4,128,2048]{2,1,0:T(8,128)(2,1)}), bf16[4,128,2048]{2,1,0:T(8,128)(2,1)}, u32[]{:S(2)}, u32[]{:S(2)}) %all-to-all-start) | async-done | bytes 2097184 | tf_op jit(solution)/shard_map/all_to_all | solution.py:28
  62.5 5.5 %fusion.6.raw_ref = f32[512,1024]{1,0:T(8,128)S(1)} fusion(bf16[512,2048]{1,0:T(8,128)(2,1)} %bitcast.17, bf16[1024,512]{1,0:T(8,128)(2,1)} %collective-permute-done.1, bf16[1024,512]{1,0:T(8,128)(2,1)} %all-gather.4.cloned.1.call-done, bf16[2048,512]{1,0:T(8,128)(2,1)} %bitcast.239), kind=kOutput, calls=%fused_computation.40 | convolution fusion | flops 2160066560 | bytes 8388608 | tf_op jit(solution)/shard_map/dot_general | solution.py:383
  71.0 16.0 %all_gather.13 = bf16[1024,256]{1,0:T(8,128)(2,1)S(1)} all-gather(bf16[256,256]{1,0:T(8,128)(2,1)} %collective-permute-done.3), channel_id=1, replica_groups=mesh['x'=4,'ylo'=2,'core'=2,'z'=4,'yhi'=2] {'x'}, dimensions={0}, use_global_device_ids=true | all-gather | bytes 655360 | tf_op jit(solution)/shard_map/all_gather | solution.py:49
  87.3 4.8 attention.1
  92.1 2.7 convolution_convert_fusion.5
  94.8 4.5 all-to-all-start.1
  99.3 4.7 copy.270
  104.1 3.3 select_bitcast_fusion
  113.8 3.8 pad_maximum_fusion.4
  117.5 4.8 collective-permute-done.7
  122.3 4.2 all-to-all-done.1
  126.6 2.2 convert_reduce_fusion.3
  131.9 4.4 all-to-all-start.2
  136.3 3.2 fusion.2
  139.6 3.2 fusion.74
  142.8 3.2 pad_maximum_fusion.1
  147.9 15.0 %all-to-all-done.2 = bf16[4,128,2048]{2,1,0:T(8,128)(2,1)} async-done(((bf16[4,128,2048]{2,1,0:T(8,128)(2,1)}), bf16[4,128,2048]{2,1,0:T(8,128)(2,1)}, u32[]{:S(2)}, u32[]{:S(2)}) %all-to-all-start.2) | async-done | bytes 2097184 | tf_op jit(solution)/shard_map/all_to_all | solution.py:28
  162.8 2.6 broadcast_in_dim.49
  165.5 4.7 all-to-all-start.4
  170.2 12.3 %fusion.1 = f32[512,3072]{1,0:T(8,128)S(1)} fusion(bf16[512,2048]{1,0:T(8,128)(2,1)} %bitcast.43, bf16[1024,1536]{1,0:T(8,128)(2,1)} %collective-permute-done.6, bf16[1024,1536]{1,0:T(8,128)(2,1)} %all-gather.6.cloned.1.call-done, bf16[2048,1536]{1,0:T(8,128)(2,1)} %bitcast.223), kind=kOutput, calls=%fused_computation.9 | convolution fusion | flops 6480199680 | bytes 20971520 | tf_op jit(solution)/shard_map/dot_general | solution.py:394
  182.4 2.7 fusion.49
  185.1 10.6 %all-to-all-done.4 = bf16[4,128,2048]{2,1,0:T(8,128)(2,1)} async-done(((bf16[4,128,2048]{2,1,0:T(8,128)(2,1)}), bf16[4,128,2048]{2,1,0:T(8,128)(2,1)}, u32[]{:S(2)}, u32[]{:S(2)}) %all-to-all-start.4) | async-done | bytes 2097184 | tf_op jit(solution)/shard_map/all_to_all | solution.py:28
  195.8 10.8 %multiply_convert_fusion.1 = (bf16[512,1536]{1,0:T(8,128)(2,1)S(1)}, bf16[512,1536]{1,0:T(8,128)(2,1)}, bf16[512,1536]{1,0:T(8,128)(2,1)S(1)}) fusion(f32[512,768]{1,0:T(8,128)} %get-tuple-element.101, f32[512,768]{1,0:T(8,128)} %get-tuple-element.102, f32[512,768]{1,0:T(8,128)} %get-tuple-element.103, f32[512,768]{1,0:T(8,128)} %get-tuple-element.100, ...), kind=kOutput, calls=%fused_computation.25 | convolution fusion | flops 3253469184 | bytes 19398656 | tf_op jit(solution)/shard_map/dot_general | solution.py:23
  209.1 13.7 %fusion.4 = bf16[512,2048]{1,0:T(8,128)(2,1)} fusion(bf16[1024,1536]{1,0:T(8,128)(2,1)} %collective-permute-done.6, bf16[1024,1536]{1,0:T(8,128)(2,1)} %all-gather.6.cloned.1.call-done, bf16[2048,1536]{1,0:T(8,128)(2,1)} %bitcast.224, bf16[512,768]{1,0:T(8,128)(2,1)} %get-tuple-element.113, bf16[512,768]{1,0:T(8,128)(2,1)} %get-tuple-element.111, ...), kind=kOutput, calls=%fused_computation.32 | convolution fusion | flops 6493831168 | bytes 17825792 | tf_op jit(solution)/shard_map/dot_general | solution.py:23
  222.8 28.8 %all_to_all.55 = bf16[4,128,2048]{2,1,0:T(8,128)(2,1)S(1)} all-to-all(bf16[4,128,2048]{2,1,0:T(8,128)(2,1)} %bitcast.244), channel_id=1, replica_groups=mesh['x'=4,'ylo'=2,'core'=2,'z'=4,'yhi'=2] {'z'}, dimensions={0} | all-to-all | bytes 4194304 | tf_op jit(solution)/shard_map/all_to_all | solution.py:34
  254.8 4.4 all-to-all-start.6
  259.3 5.2 %convolution_convert_fusion.1 = bf16[1024,1536]{1,0:T(8,128)(2,1)} fusion(bf16[512,1536]{1,0:T(8,128)(2,1)} %get-tuple-element.98, bf16[512,2048]{1,0:T(8,128)(2,1)} %bitcast.71), kind=kOutput, calls=%fused_computation.16 | convolution fusion | flops 1612185600 | bytes 5767168 | tf_op jit(solution)/shard_map/dot_general | solution.py:23
  264.6 18.5 %all-to-all-done.6 = bf16[4,128,2048]{2,1,0:T(8,128)(2,1)} async-done(((bf16[4,128,2048]{2,1,0:T(8,128)(2,1)}), bf16[4,128,2048]{2,1,0:T(8,128)(2,1)}, u32[]{:S(2)}, u32[]{:S(2)}) %all-to-all-start.6) | async-done | bytes 2097184 | tf_op jit(solution)/shard_map/all_to_all | solution.py:28
  283.1 2.2 convolution_convert_fusion.7
  289.4 6.2 %add_convert_fusion.1 = bf16[1024,1536]{1,0:T(8,128)(2,1)} fusion(bf16[1024,1536]{1,0:T(8,128)(2,1)} %collective-permute-done.22, bf16[512,1536]{1,0:T(8,128)(2,1)} %get-tuple-element.98, bf16[512,2048]{1,0:T(8,128)(2,1)} %bitcast.71), kind=kOutput, calls=%fused_computation.5 | convolution fusion | flops 1618477056 | bytes 8912896 | tf_op jit(solution)/shard_map/dot_general | solution.py:23
  295.8 3.5 convolution_convert_fusion.9.dctx_ref
  299.4 6.0 %attention_back.1 = (bf16[512,512]{1,0:T(8,128)(2,1)S(1)}, f32[512,512]{1,0:T(8,128)S(1)}, bf16[512,512]{1,0:T(8,128)(2,1)S(1)}, f32[1,128]{1,0:T(1,128)S(1)}) custom-call(s32[1]{0:T(128)} %bitcast.9.y_ref, bf16[512,512]{1,0:T(8,128)(2,1)S(1)} %get-tuple-element.23.q_ref, bf16[512,512]{1,0:T(8,128)(2,1)S(1)} %copy-done.5, bf16[512,512]{1,0:T(8,128)(2,1)S(1)} %copy-done.7, ...), custom_call_target="tpu_custom_call" | custom-call | flops 2200000000 | bytes 7000000 | tf_op jit(solution)/shard_map/attention_back/pallas_call | solution.py:249
  307.2 7.1 %convolution_convert_fusion = bf16[1024,3072]{1,0:T(8,128)(2,1)} fusion(bf16[512,2048]{1,0:T(8,128)(2,1)} %bitcast.43, bf16[512,768]{1,0:T(8,128)(2,1)S(1)} %copy-done.33, bf16[512,768]{1,0:T(8,128)(2,1)S(1)} %copy-done.31, bf16[512,768]{1,0:T(8,128)(2,1)S(1)} %copy-done.32, bf16[512,768]{1,0:T(8,128)(2,1)S(1)} %copy-done.30), kind=kOutput, calls=%fused_computation.7 | convolution fusion | flops 3236954112 | bytes 10485760 | tf_op jit(solution)/shard_map/dot_general | solution.py:23
  314.4 6.5 %collective-permute-done.9.got_ref = bf16[512,512]{1,0:T(8,128)(2,1)S(1)} collective-permute-done((bf16[512,512]{1,0:T(8,128)(2,1)S(1)}, bf16[512,512]{1,0:T(8,128)(2,1)S(1)}, u32[]{:S(2)}, u32[]{:S(2)}) %collective-permute-start.9) | collective-permute-done | bytes 524320 | tf_op jit(solution)/shard_map/ppermute | solution.py:39
  321.7 2.9 convolution_convert_fusion.6
  325.0 2.5 fusion.15
  329.1 2.3 add_convert_fusion.2
  331.5 10.3 %add_convert_fusion = bf16[1024,3072]{1,0:T(8,128)(2,1)} fusion(bf16[1024,3072]{1,0:T(8,128)(2,1)} %collective-permute-done.14, bf16[512,2048]{1,0:T(8,128)(2,1)} %bitcast.43, bf16[512,768]{1,0:T(8,128)(2,1)} %get-tuple-element.113, bf16[512,768]{1,0:T(8,128)(2,1)} %get-tuple-element.111, bf16[512,768]{1,0:T(8,128)(2,1)} %get-tuple-element.112, ...), kind=kOutput, calls=%fused_computation.1 | convolution fusion | flops 3249537024 | bytes 16777216 | tf_op jit(solution)/shard_map/dot_general | solution.py:23
  343.2 7.8 %convolution_convert_fusion.4 = bf16[512,2048]{1,0:T(8,128)(2,1)} fusion(bf16[512,1536]{1,0:T(8,128)(2,1)} %get-tuple-element.98, bf16[1024,768]{1,0:T(8,128)(2,1)} %collective-permute-done.8, bf16[1024,768]{1,0:T(8,128)(2,1)S(1)} %copy-done.43, bf16[2048,768]{1,0:T(8,128)(2,1)} %bitcast.236), kind=kOutput, calls=%fused_computation.30 | convolution fusion | flops 3241148416 | bytes 9961472 | tf_op jit(solution)/shard_map/dot_general | solution.py:23
  351.0 4.6 all-to-all-start.3
  358.3 24.2 %all-to-all-done.3 = bf16[4,128,2048]{2,1,0:T(8,128)(2,1)} async-done(((bf16[4,128,2048]{2,1,0:T(8,128)(2,1)}), bf16[4,128,2048]{2,1,0:T(8,128)(2,1)}, u32[]{:S(2)}, u32[]{:S(2)}) %all-to-all-start.3) | async-done | bytes 2097184 | tf_op jit(solution)/shard_map/all_to_all | solution.py:34
  382.5 4.9 all-to-all-start.8
  387.5 5.7 %convolution_convert_fusion.3 = bf16[512,2048]{1,0:T(8,128)(2,1)} fusion(bf16[512,1024]{1,0:T(8,128)(2,1)S(1)} %copy-done.3, bf16[1024,512]{1,0:T(8,128)(2,1)} %collective-permute-done.1, bf16[1024,512]{1,0:T(8,128)(2,1)S(1)} %copy-done.44, bf16[2048,512]{1,0:T(8,128)(2,1)} %bitcast.240), kind=kOutput, calls=%fused_computation.29 | convolution fusion | flops 2161115136 | bytes 7340032 | tf_op jit(solution)/shard_map/dot_general | solution.py:23
  393.4 4.8 all-to-all-start.7
  404.3 2.1 convert_reduce_fusion.2
  408.4 3.3 multiply_add_fusion
  413.3 12.0 %all-to-all-done.7 = bf16[4,128,2048]{2,1,0:T(8,128)(2,1)} async-done(((bf16[4,128,2048]{2,1,0:T(8,128)(2,1)}), bf16[4,128,2048]{2,1,0:T(8,128)(2,1)}, u32[]{:S(2)}, u32[]{:S(2)}) %all-to-all-start.7) | async-done | bytes 2097184 | tf_op jit(solution)/shard_map/all_to_all | solution.py:34
  425.3 2.1 convert_reduce_fusion
  429.4 2.2 fusion.21
  452.7 2.5 collective-permute-done.12
  460.3 2.2 collective-permute-start.16
  464.7 5.7 %collective-permute-done.15 = bf16[128,1536]{1,0:T(8,128)(2,1)S(1)} collective-permute-done((bf16[128,1536]{1,0:T(8,128)(2,1)S(1)}, bf16[128,1536]{1,0:T(8,128)(2,1)S(1)}, u32[]{:S(2)}, u32[]{:S(2)}) %collective-permute-start.15) | collective-permute-done | bytes 393248 | tf_op jit(solution)/shard_map/ppermute | solution.py:39
  471.8 8.2 %collective-permute-done.17 = bf16[128,1536]{1,0:T(8,128)(2,1)S(1)} collective-permute-done((bf16[128,1536]{1,0:T(8,128)(2,1)S(1)}, bf16[128,1536]{1,0:T(8,128)(2,1)S(1)}, u32[]{:S(2)}, u32[]{:S(2)}) %collective-permute-start.17) | collective-permute-done | bytes 393248 | tf_op jit(solution)/shard_map/ppermute | solution.py:43
  483.5 3.3 all-to-all-start.9
  487.7 6.8 %all-to-all-done.9 = f32[8,1,272]{2,1,0:T(1,128)S(1)} async-done(((f32[8,1,272]{2,1,0:T(1,128)}), f32[8,1,272]{2,1,0:T(1,128)S(1)}, u32[]{:S(2)}, u32[]{:S(2)}) %all-to-all-start.9) | async-done | bytes 8736 | tf_op jit(solution)/shard_map/all_to_all | solution.py:446
  (267 shorter events, 98.7 us)
Async XLA Ops:
  7.2 46.6 %all-gather.4.cloned.1.call-start = ((), (), s32[]{:S(2)}) async-start(), calls=%async_computation.14 | async-start | bytes 1310720 | tf_op jit(solution)/shard_map/all_gather | solution.py:49
  7.2 5.8 %copy-start.24 = (bf16[2048,768]{1,0:T(8,128)(2,1)S(1)}, bf16[2048,768]{1,0:T(8,128)(2,1)}, u32[]{:S(2)}) copy-start(bf16[2048,768]{1,0:T(8,128)(2,1)} %param.26) | copy-start | bytes 9437188
  10.0 17.4 %collective-permute-start = (bf16[256,512]{1,0:T(8,128)(2,1)}, bf16[256,512]{1,0:T(8,128)(2,1)}, u32[]{:S(2)}, u32[]{:S(2)}) collective-permute-start(bf16[256,512]{1,0:T(8,128)(2,1)} %constant_dynamic-slice_fusion.7), channel_id=1, source_target_pairs={{0,17},{17,0},{1,16},{16,1},{2,19},{19,2},{3,18},{18,3},{4,21},{21... | collective-permute-start | bytes 786440 | tf_op jit(solution)/shard_map/ppermute | solution.py:43
  19.1 26.4 %collective-permute-start.5 = (bf16[256,1536]{1,0:T(8,128)(2,1)}, bf16[256,1536]{1,0:T(8,128)(2,1)}, u32[]{:S(2)}, u32[]{:S(2)}) collective-permute-start(bf16[256,1536]{1,0:T(8,128)(2,1)} %constant_dynamic-slice_fusion.5), channel_id=1, source_target_pairs={{0,17},{17,0},{1,16},{16,1},{2,19},{19,2},{3,18},{18,3},{4,21},{21... | collective-permute-start | bytes 2359304 | tf_op jit(solution)/shard_map/ppermute | solution.py:43
  21.6 5.7 %copy-start.40 = (f32[2048]{0:T(1024)S(1)}, f32[2048]{0:T(1024)}, u32[]{:S(2)}) copy-start(f32[2048]{0:T(1024)} %param.17) | copy-start | bytes 24580
  31.0 31.5 %all-to-all-start = ((bf16[4,128,2048]{2,1,0:T(8,128)(2,1)}), bf16[4,128,2048]{2,1,0:T(8,128)(2,1)}, u32[]{:S(2)}, u32[]{:S(2)}) async-start(bf16[4,128,2048]{2,1,0:T(8,128)(2,1)} %broadcast_in_dim.43), calls=%async_computation | async-start | bytes 4194304 | tf_op jit(solution)/shard_map/all_to_all | solution.py:28
  36.4 8.9 %copy-start.46 = (s32[1,3]{1,0:T(1,128)S(1)}, s32[1,3]{1,0:T(1,128)}, u32[]{:S(2)}) copy-start(s32[1,3]{1,0:T(1,128)} %param.16) | copy-start | bytes 40
  36.4 77.2 %all-gather.6.cloned.1.call-start = ((), (), s32[]{:S(2)}) async-start(), calls=%async_computation.15 | async-start | bytes 3932160 | tf_op jit(solution)/shard_map/all_gather | solution.py:49
  42.3 28.7 %collective-permute-start.3 = (bf16[256,256]{1,0:T(8,128)(2,1)}, bf16[256,256]{1,0:T(8,128)(2,1)}, u32[]{:S(2)}, u32[]{:S(2)}) collective-permute-start(bf16[256,256]{1,0:T(8,128)(2,1)} %constant_dynamic-slice_fusion.6), channel_id=1, source_target_pairs={{0,17},{17,0},{1,16},{16,1},{2,19},{19,2},{3,18},{18,3},{4,21},{21... | collective-permute-start | bytes 393224 | tf_op jit(solution)/shard_map/ppermute | solution.py:43
  53.8 8.7 %collective-permute-start.1 = (bf16[1024,512]{1,0:T(8,128)(2,1)}, bf16[1024,512]{1,0:T(8,128)(2,1)}, u32[]{:S(2)}, u32[]{:S(2)}) collective-permute-start(bf16[1024,512]{1,0:T(8,128)(2,1)} %all-gather.4.cloned.1.call-done), channel_id=1, source_target_pairs={{0,8},{8,0},{1,9},{9,1},{2,10},{10,2},{3,11},{11,3},{4,12},{12,4},... | collective-permute-start | bytes 3145736 | tf_op jit(solution)/shard_map/ppermute | solution.py:39
  62.5 5.5 %copy-start = (f32[128]{0:T(128)S(1)}, f32[128]{0:T(128)}, u32[]{:S(2)}) copy-start(f32[128]{0:T(128)} %param.20) | copy-start | bytes 1540
  62.5 5.5 %copy-start.1 = (f32[128]{0:T(128)S(1)}, f32[128]{0:T(128)}, u32[]{:S(2)}) copy-start(f32[128]{0:T(128)} %param.19) | copy-start | bytes 1540
  68.0 19.1 %copy-start.26 = (bf16[8,1,128,256]{3,2,1,0:T(8,128)(2,1)S(1)}, bf16[8,1,128,256]{3,2,1,0:T(8,128)(2,1)}, u32[]{:S(2)}) copy-start(bf16[8,1,128,256]{3,2,1,0:T(8,128)(2,1)} %copy-done.25) | copy-start | bytes 1572868
  68.0 19.1 %copy-start.27 = (bf16[8,128,256]{2,1,0:T(8,128)(2,1)S(1)}, bf16[8,128,256]{2,1,0:T(8,128)(2,1)}, u32[]{:S(2)}) copy-start(bf16[8,128,256]{2,1,0:T(8,128)(2,1)} %get-tuple-element.114) | copy-start | bytes 1572868
  69.2 25.6 %copy-start.4 = (bf16[512,512]{1,0:T(8,128)(2,1)}, bf16[512,512]{1,0:T(8,128)(2,1)S(1)}, u32[]{:S(2)}) copy-start(bf16[512,512]{1,0:T(8,128)(2,1)S(1)} %get-tuple-element.24.kv_ref) | copy-start | bytes 1572868
  69.2 18.0 %collective-permute-start.2 = (bf16[512,512]{1,0:T(8,128)(2,1)S(1)}, bf16[512,512]{1,0:T(8,128)(2,1)S(1)}, u32[]{:S(2)}, u32[]{:S(2)}) collective-permute-start(bf16[512,512]{1,0:T(8,128)(2,1)S(1)} %get-tuple-element.24.kv_ref), channel_id=1, source_target_pairs={{0,1},{1,0},{2,3},{3,2},{4,5},{5,4},{6,7},{7,6},{8,9},{9,8},{10,11... | collective-permute-start | bytes 1572872 | tf_op jit(solution)/shard_map/ppermute | solution.py:39
  86.9 7.8 %copy-start.34 = (bf16[1024,256]{1,0:T(8,128)(2,1)}, bf16[1024,256]{1,0:T(8,128)(2,1)S(1)}, u32[]{:S(2)}) copy-start(bf16[1024,256]{1,0:T(8,128)(2,1)S(1)} %all_gather.13) | copy-start | bytes 1572868
  86.9 5.1 %collective-permute-start.4 = (bf16[1024,256]{1,0:T(8,128)(2,1)S(1)}, bf16[1024,256]{1,0:T(8,128)(2,1)S(1)}, u32[]{:S(2)}, u32[]{:S(2)}) collective-permute-start(bf16[1024,256]{1,0:T(8,128)(2,1)S(1)} %all_gather.13), channel_id=1, source_target_pairs={{0,8},{8,0},{1,9},{9,1},{2,10},{10,2},{3,11},{11,3},{4,12},{12,4},... | collective-permute-start | bytes 1572872 | tf_op jit(solution)/shard_map/ppermute | solution.py:39
  87.2 7.6 %copy-start.28 = (bf16[16,128,256]{2,1,0:T(8,128)(2,1)}, bf16[16,128,256]{2,1,0:T(8,128)(2,1)S(1)}, u32[]{:S(2)}) copy-start(bf16[16,128,256]{2,1,0:T(8,128)(2,1)S(1)} %pad_maximum_fusion.8) | copy-start | bytes 3145732
  87.3 7.5 %copy-start.6 = (bf16[512,512]{1,0:T(8,128)(2,1)}, bf16[512,512]{1,0:T(8,128)(2,1)S(1)}, u32[]{:S(2)}) copy-start(bf16[512,512]{1,0:T(8,128)(2,1)S(1)} %collective-permute-done.2.other_ref) | copy-start | bytes 1572868
  94.8 31.8 %all-to-all-start.1 = ((bf16[4,128,2048]{2,1,0:T(8,128)(2,1)}), bf16[4,128,2048]{2,1,0:T(8,128)(2,1)}, u32[]{:S(2)}, u32[]{:S(2)}) async-start(bf16[4,128,2048]{2,1,0:T(8,128)(2,1)} %bitcast.242), calls=%async_computation.1 | async-start | bytes 4194304 | tf_op jit(solution)/shard_map/all_to_all | solution.py:34
  99.3 48.6 %all-gather.8.cloned.1.call-start = ((), (), s32[]{:S(2)}) async-start(), calls=%async_computation.16 | async-start | bytes 1966080 | tf_op jit(solution)/shard_map/all_gather | solution.py:49
  104.1 6.6 %copy-start.29 = (bf16[128,8,128]{0,2,1:T(8,128)(2,1)S(1)}, bf16[128,8,128]{0,2,1:T(8,128)(2,1)}, u32[]{:S(2)}) copy-start(bf16[128,8,128]{0,2,1:T(8,128)(2,1)} %get-tuple-element.127) | copy-start | bytes 786436
  109.3 13.0 %collective-permute-start.7 = (bf16[256,768]{1,0:T(8,128)(2,1)}, bf16[256,768]{1,0:T(8,128)(2,1)}, u32[]{:S(2)}, u32[]{:S(2)}) collective-permute-start(bf16[256,768]{1,0:T(8,128)(2,1)} %constant_dynamic-slice_fusion.4), channel_id=1, source_target_pairs={{0,17},{17,0},{1,16},{16,1},{2,19},{19,2},{3,18},{18,3},{4,21},{21... | collective-permute-start | bytes 1179656 | tf_op jit(solution)/shard_map/ppermute | solution.py:43
  113.6 56.6 %collective-permute-start.6 = (bf16[1024,1536]{1,0:T(8,128)(2,1)}, bf16[1024,1536]{1,0:T(8,128)(2,1)}, u32[]{:S(2)}, u32[]{:S(2)}) collective-permute-start(bf16[1024,1536]{1,0:T(8,128)(2,1)} %all-gather.6.cloned.1.call-done), channel_id=1, source_target_pairs={{0,8},{8,0},{1,9},{9,1},{2,10},{10,2},{3,11},{11,3},{4,12},{12,4},... | collective-permute-start | bytes 9437192 | tf_op jit(solution)/shard_map/ppermute | solution.py:39
  131.9 31.0 %all-to-all-start.2 = ((bf16[4,128,2048]{2,1,0:T(8,128)(2,1)}), bf16[4,128,2048]{2,1,0:T(8,128)(2,1)}, u32[]{:S(2)}, u32[]{:S(2)}) async-start(bf16[4,128,2048]{2,1,0:T(8,128)(2,1)} %broadcast_in_dim.48), calls=%async_computation.2 | async-start | bytes 4194304 | tf_op jit(solution)/shard_map/all_to_all | solution.py:28
  147.8 47.9 %collective-permute-start.8 = (bf16[1024,768]{1,0:T(8,128)(2,1)}, bf16[1024,768]{1,0:T(8,128)(2,1)}, u32[]{:S(2)}, u32[]{:S(2)}) collective-permute-start(bf16[1024,768]{1,0:T(8,128)(2,1)} %all-gather.8.cloned.1.call-done), channel_id=1, source_target_pairs={{0,8},{8,0},{1,9},{9,1},{2,10},{10,2},{3,11},{11,3},{4,12},{12,4},... | collective-permute-start | bytes 4718600 | tf_op jit(solution)/shard_map/ppermute | solution.py:39
  165.5 30.3 %all-to-all-start.4 = ((bf16[4,128,2048]{2,1,0:T(8,128)(2,1)}), bf16[4,128,2048]{2,1,0:T(8,128)(2,1)}, u32[]{:S(2)}, u32[]{:S(2)}) async-start(bf16[4,128,2048]{2,1,0:T(8,128)(2,1)} %broadcast_in_dim.49), calls=%async_computation.4 | async-start | bytes 4194304 | tf_op jit(solution)/shard_map/all_to_all | solution.py:28
  222.8 29.1 %copy-start.17 = (f32[128,2048]{1,0:T(8,128)S(1)}, f32[128,2048]{1,0:T(8,128)}, u32[]{:S(2)}) copy-start(f32[128,2048]{1,0:T(8,128)} %copy-done.16) | copy-start | bytes 3145732
  254.8 28.2 %all-to-all-start.6 = ((bf16[4,128,2048]{2,1,0:T(8,128)(2,1)}), bf16[4,128,2048]{2,1,0:T(8,128)(2,1)}, u32[]{:S(2)}, u32[]{:S(2)}) async-start(bf16[4,128,2048]{2,1,0:T(8,128)(2,1)} %broadcast_in_dim.50), calls=%async_computation.6 | async-start | bytes 4194304 | tf_op jit(solution)/shard_map/all_to_all | solution.py:28
  259.3 172.4 %reduce-scatter.9.cloned.1.call-start = ((), (), s32[]{:S(2)}) async-start(), calls=%async_computation.19 | async-start | bytes 1310720 | tf_op jit(solution)/shard_map/reduce_scatter | solution.py:58
  264.6 24.8 %collective-permute-start.22 = (bf16[1024,1536]{1,0:T(8,128)(2,1)}, bf16[1024,1536]{1,0:T(8,128)(2,1)}, u32[]{:S(2)}, u32[]{:S(2)}) collective-permute-start(bf16[1024,1536]{1,0:T(8,128)(2,1)} %convolution_convert_fusion.1), channel_id=1, source_target_pairs={{0,8},{8,0},{1,9},{9,1},{2,10},{10,2},{3,11},{11,3},{4,12},{12,4},... | collective-permute-start | bytes 9437192 | tf_op jit(solution)/shard_map/ppermute | solution.py:39
  285.3 2.7 collective-permute-start.18
  289.3 152.5 %reduce-scatter.11.cloned.1.call-start = ((), (), s32[]{:S(2)}) async-start(), calls=%async_computation.20 | async-start | bytes 3932160 | tf_op jit(solution)/shard_map/reduce_scatter | solution.py:58
  295.6 147.6 %reduce-scatter.5.cloned.1.call-start = ((), (), s32[]{:S(2)}) async-start(), calls=%async_computation.17 | async-start | bytes 2621440 | tf_op jit(solution)/shard_map/reduce_scatter | solution.py:58
  299.4 7.9 %copy-start.30 = (bf16[512,768]{1,0:T(8,128)(2,1)S(1)}, bf16[512,768]{1,0:T(8,128)(2,1)}, u32[]{:S(2)}) copy-start(bf16[512,768]{1,0:T(8,128)(2,1)} %get-tuple-element.110) | copy-start | bytes 2359300
  299.4 7.9 %copy-start.31 = (bf16[512,768]{1,0:T(8,128)(2,1)S(1)}, bf16[512,768]{1,0:T(8,128)(2,1)}, u32[]{:S(2)}) copy-start(bf16[512,768]{1,0:T(8,128)(2,1)} %get-tuple-element.111) | copy-start | bytes 2359300
  299.4 7.9 %copy-start.32 = (bf16[512,768]{1,0:T(8,128)(2,1)S(1)}, bf16[512,768]{1,0:T(8,128)(2,1)}, u32[]{:S(2)}) copy-start(bf16[512,768]{1,0:T(8,128)(2,1)} %get-tuple-element.112) | copy-start | bytes 2359300
  299.4 7.8 %copy-start.33 = (bf16[512,768]{1,0:T(8,128)(2,1)S(1)}, bf16[512,768]{1,0:T(8,128)(2,1)}, u32[]{:S(2)}) copy-start(bf16[512,768]{1,0:T(8,128)(2,1)} %get-tuple-element.113) | copy-start | bytes 2359300
  305.4 15.6 %collective-permute-start.9 = (bf16[512,512]{1,0:T(8,128)(2,1)S(1)}, bf16[512,512]{1,0:T(8,128)(2,1)S(1)}, u32[]{:S(2)}, u32[]{:S(2)}) collective-permute-start(bf16[512,512]{1,0:T(8,128)(2,1)S(1)} %get-tuple-element.28), channel_id=1, source_target_pairs={{0,1},{1,0},{2,3},{3,2},{4,5},{5,4},{6,7},{7,6},{8,9},{9,8},{10,11... | collective-permute-start | bytes 1572872 | tf_op jit(solution)/shard_map/ppermute | solution.py:39
  314.4 17.1 %collective-permute-start.14 = (bf16[1024,3072]{1,0:T(8,128)(2,1)}, bf16[1024,3072]{1,0:T(8,128)(2,1)}, u32[]{:S(2)}, u32[]{:S(2)}) collective-permute-start(bf16[1024,3072]{1,0:T(8,128)(2,1)} %convolution_convert_fusion), channel_id=1, source_target_pairs={{0,8},{8,0},{1,9},{9,1},{2,10},{10,2},{3,11},{11,3},{4,12},{12,4},... | collective-permute-start | bytes 18874376 | tf_op jit(solution)/shard_map/ppermute | solution.py:39
  324.6 4.5 collective-permute-start.10
  331.4 125.3 %reduce-scatter.7.cloned.1.call-start = ((), (), s32[]{:S(2)}) async-start(), calls=%async_computation.18 | async-start | bytes 7864320 | tf_op jit(solution)/shard_map/reduce_scatter | solution.py:58
  351.0 36.5 %copy-start.3 = (bf16[512,1024]{1,0:T(8,128)(2,1)S(1)}, bf16[512,1024]{1,0:T(8,128)(2,1)}, u32[]{:S(2)}) copy-start(bf16[512,1024]{1,0:T(8,128)(2,1)} %copy-done.2) | copy-start | bytes 3145732
  351.0 36.5 %copy-start.44 = (bf16[1024,512]{1,0:T(8,128)(2,1)S(1)}, bf16[1024,512]{1,0:T(8,128)(2,1)}, u32[]{:S(2)}) copy-start(bf16[1024,512]{1,0:T(8,128)(2,1)} %all-gather.4.cloned.1.call-done) | copy-start | bytes 3145732
  351.0 31.5 %all-to-all-start.3 = ((bf16[4,128,2048]{2,1,0:T(8,128)(2,1)}), bf16[4,128,2048]{2,1,0:T(8,128)(2,1)}, u32[]{:S(2)}, u32[]{:S(2)}) async-start(bf16[4,128,2048]{2,1,0:T(8,128)(2,1)} %bitcast.243), calls=%async_computation.3 | async-start | bytes 4194304 | tf_op jit(solution)/shard_map/all_to_all | solution.py:34
  382.5 10.9 %all-to-all-start.8 = ((f32[16,1,16]{2,1,0:T(1,128)}), f32[16,1,16]{2,1,0:T(1,128)S(1)}, u32[]{:S(2)}, u32[]{:S(2)}) async-start(f32[16,1,16]{2,1,0:T(1,128)} %bitcast.89), calls=%async_computation.10 | async-start | bytes 16384 | tf_op jit(solution)/shard_map/all_to_all | solution.py:443
  393.4 31.8 %all-to-all-start.7 = ((bf16[4,128,2048]{2,1,0:T(8,128)(2,1)}), bf16[4,128,2048]{2,1,0:T(8,128)(2,1)}, u32[]{:S(2)}, u32[]{:S(2)}) async-start(bf16[4,128,2048]{2,1,0:T(8,128)(2,1)} %bitcast.241), calls=%async_computation.7 | async-start | bytes 4194304 | tf_op jit(solution)/shard_map/all_to_all | solution.py:34
  413.2 15.9 %copy-start.14 = (f32[128,2048]{1,0:T(8,128)S(1)}, f32[128,2048]{1,0:T(8,128)}, u32[]{:S(2)}) copy-start(f32[128,2048]{1,0:T(8,128)} %copy.300) | copy-start | bytes 3145732
  413.2 15.9 %copy-start.37 = (f32[2048]{0:T(1024)S(1)}, f32[2048]{0:T(1024)}, u32[]{:S(2)}) copy-start(f32[2048]{0:T(1024)} %copy-done.36) | copy-start | bytes 24580
  413.2 15.9 %copy-start.42 = (f32[128]{0:T(128)S(1)}, f32[128]{0:T(128)}, u32[]{:S(2)}) copy-start(f32[128]{0:T(128)} %copy-done.41) | copy-start | bytes 1540
  432.8 5.9 %collective-permute-start.19 = (bf16[128,256]{0,1:T(8,128)(2,1)S(1)}, bf16[128,256]{0,1:T(8,128)(2,1)S(1)}, u32[]{:S(2)}, u32[]{:S(2)}) collective-permute-start(bf16[128,256]{0,1:T(8,128)(2,1)S(1)} %get-tuple-element.136), channel_id=1, source_target_pairs={{0,16},{16,0},{1,17},{17,1},{2,18},{18,2},{3,19},{19,3},{4,20},{20... | collective-permute-start | bytes 196616 | tf_op jit(solution)/shard_map/ppermute | solution.py:39
  434.6 5.5 %collective-permute-start.21 = (bf16[128,256]{0,1:T(8,128)(2,1)S(1)}, bf16[128,256]{0,1:T(8,128)(2,1)S(1)}, u32[]{:S(2)}, u32[]{:S(2)}) collective-permute-start(bf16[128,256]{0,1:T(8,128)(2,1)S(1)} %get-tuple-element.137), channel_id=1, source_target_pairs={{0,17},{17,0},{1,16},{16,1},{2,19},{19,2},{3,18},{18,3},{4,21},{21... | collective-permute-start | bytes 196616 | tf_op jit(solution)/shard_map/ppermute | solution.py:43
  435.3 5.8 %collective-permute-start.20 = (bf16[128,256]{0,1:T(8,128)(2,1)S(1)}, bf16[128,256]{0,1:T(8,128)(2,1)S(1)}, u32[]{:S(2)}, u32[]{:S(2)}) collective-permute-start(bf16[128,256]{0,1:T(8,128)(2,1)S(1)} %slice.306), channel_id=1, source_target_pairs={{0,1},{1,0},{2,3},{3,2},{4,5},{5,4},{6,7},{7,6},{8,9},{9,8},{10,11... | collective-permute-start | bytes 196616 | tf_op jit(solution)/shard_map/ppermute | solution.py:39
  444.3 7.4 %collective-permute-start.11 = (bf16[128,512]{1,0:T(8,128)(2,1)S(1)}, bf16[128,512]{1,0:T(8,128)(2,1)S(1)}, u32[]{:S(2)}, u32[]{:S(2)}) collective-permute-start(bf16[128,512]{1,0:T(8,128)(2,1)S(1)} %get-tuple-element.134), channel_id=1, source_target_pairs={{0,16},{16,0},{1,17},{17,1},{2,18},{18,2},{3,19},{19,3},{4,20},{20... | collective-permute-start | bytes 393224 | tf_op jit(solution)/shard_map/ppermute | solution.py:39
  445.4 7.3 %collective-permute-start.13 = (bf16[128,512]{1,0:T(8,128)(2,1)S(1)}, bf16[128,512]{1,0:T(8,128)(2,1)S(1)}, u32[]{:S(2)}, u32[]{:S(2)}) collective-permute-start(bf16[128,512]{1,0:T(8,128)(2,1)S(1)} %get-tuple-element.135), channel_id=1, source_target_pairs={{0,17},{17,0},{1,16},{16,1},{2,19},{19,2},{3,18},{18,3},{4,21},{21... | collective-permute-start | bytes 393224 | tf_op jit(solution)/shard_map/ppermute | solution.py:43
  447.2 8.0 %collective-permute-start.12 = (bf16[128,512]{1,0:T(8,128)(2,1)S(1)}, bf16[128,512]{1,0:T(8,128)(2,1)S(1)}, u32[]{:S(2)}, u32[]{:S(2)}) collective-permute-start(bf16[128,512]{1,0:T(8,128)(2,1)S(1)} %slice.289), channel_id=1, source_target_pairs={{0,1},{1,0},{2,3},{3,2},{4,5},{5,4},{6,7},{7,6},{8,9},{9,8},{10,11... | collective-permute-start | bytes 393224 | tf_op jit(solution)/shard_map/ppermute | solution.py:39
  448.7 38.2 %collective-permute-start.23 = (bf16[128,768]{0,1:T(8,128)(2,1)S(1)}, bf16[128,768]{0,1:T(8,128)(2,1)S(1)}, u32[]{:S(2)}, u32[]{:S(2)}) collective-permute-start(bf16[128,768]{0,1:T(8,128)(2,1)S(1)} %get-tuple-element.128), channel_id=1, source_target_pairs={{0,16},{16,0},{1,17},{17,1},{2,18},{18,2},{3,19},{19,3},{4,20},{20... | collective-permute-start | bytes 589832 | tf_op jit(solution)/shard_map/ppermute | solution.py:39
  449.7 37.2 %collective-permute-start.25 = (bf16[128,768]{0,1:T(8,128)(2,1)S(1)}, bf16[128,768]{0,1:T(8,128)(2,1)S(1)}, u32[]{:S(2)}, u32[]{:S(2)}) collective-permute-start(bf16[128,768]{0,1:T(8,128)(2,1)S(1)} %get-tuple-element.129), channel_id=1, source_target_pairs={{0,17},{17,0},{1,16},{16,1},{2,19},{19,2},{3,18},{18,3},{4,21},{21... | collective-permute-start | bytes 589832 | tf_op jit(solution)/shard_map/ppermute | solution.py:43
  458.3 12.1 %collective-permute-start.15 = (bf16[128,1536]{1,0:T(8,128)(2,1)S(1)}, bf16[128,1536]{1,0:T(8,128)(2,1)S(1)}, u32[]{:S(2)}, u32[]{:S(2)}) collective-permute-start(bf16[128,1536]{1,0:T(8,128)(2,1)S(1)} %get-tuple-element.120), channel_id=1, source_target_pairs={{0,16},{16,0},{1,17},{17,1},{2,18},{18,2},{3,19},{19,3},{4,20},{20... | collective-permute-start | bytes 1179656 | tf_op jit(solution)/shard_map/ppermute | solution.py:39
  459.1 20.9 %collective-permute-start.17 = (bf16[128,1536]{1,0:T(8,128)(2,1)S(1)}, bf16[128,1536]{1,0:T(8,128)(2,1)S(1)}, u32[]{:S(2)}, u32[]{:S(2)}) collective-permute-start(bf16[128,1536]{1,0:T(8,128)(2,1)S(1)} %get-tuple-element.121), channel_id=1, source_target_pairs={{0,17},{17,0},{1,16},{16,1},{2,19},{19,2},{3,18},{18,3},{4,21},{21... | collective-permute-start | bytes 1179656 | tf_op jit(solution)/shard_map/ppermute | solution.py:43
  460.3 19.7 %collective-permute-start.16 = (bf16[128,1536]{1,0:T(8,128)(2,1)S(1)}, bf16[128,1536]{1,0:T(8,128)(2,1)S(1)}, u32[]{:S(2)}, u32[]{:S(2)}) collective-permute-start(bf16[128,1536]{1,0:T(8,128)(2,1)S(1)} %slice.298), channel_id=1, source_target_pairs={{0,1},{1,0},{2,3},{3,2},{4,5},{5,4},{6,7},{7,6},{8,9},{9,8},{10,11... | collective-permute-start | bytes 1179656 | tf_op jit(solution)/shard_map/ppermute | solution.py:39
  470.4 16.5 %collective-permute-start.24 = (bf16[128,768]{0,1:T(8,128)(2,1)S(1)}, bf16[128,768]{0,1:T(8,128)(2,1)S(1)}, u32[]{:S(2)}, u32[]{:S(2)}) collective-permute-start(bf16[128,768]{0,1:T(8,128)(2,1)S(1)} %slice.312), channel_id=1, source_target_pairs={{0,1},{1,0},{2,3},{3,2},{4,5},{5,4},{6,7},{7,6},{8,9},{9,8},{10,11... | collective-permute-start | bytes 589832 | tf_op jit(solution)/shard_map/ppermute | solution.py:39
  483.5 11.0 %all-to-all-start.9 = ((f32[8,1,272]{2,1,0:T(1,128)}), f32[8,1,272]{2,1,0:T(1,128)S(1)}, u32[]{:S(2)}, u32[]{:S(2)}) async-start(f32[8,1,272]{2,1,0:T(1,128)} %broadcast_in_dim.51), calls=%async_computation.11 | async-start | bytes 24576 | tf_op jit(solution)/shard_map/all_to_all | solution.py:446
  (25 other events, 63.3 us)
Sparse Core Ops, SparseCore 0:
  27.5 26.2 all-gather.3
  55.4 44.0 all-gather.5
  122.5 25.3 all-gather.7
  289.5 20.9 reduce-scatter.8
  312.9 37.9 reduce-scatter.10
  353.3 29.3 reduce-scatter.4
  385.1 63.6 reduce-scatter.6
